TPU v7x, 128 devices: a whole 4x4x4 slice. The times are simulated.
128 devices in a mesh: seq: 64 (over y_lo, x, z, core), head: 2 (over y_hi).
Axes of the slice: x: 4, y: 4 (y_hi: 2, y_lo: 2; y = y_hi * 2 + y_lo), z: 4, core: 2. Of those that a mesh axis runs over, the one named last changes fastest.
Arguments:
- ctx_hidden: bfloat16 [32768, 5120], P('seq', 'head'), may hold values from -1200 to 1200
- fin_hidden: bfloat16 [1024, 5120], P('seq', 'head'), may hold values from -1200 to 1200
- lengths: int32 [64], replicated, may hold values from 1 to 512, 24576 in all
- ln_gain: float32 [5120], P('head'), may hold values from 0.1 to 1.9
- q_weight: bfloat16 [5120, 2560], P(None, 'head'), may hold values from -0.078125 to 0.078125
- k_weight: bfloat16 [5120, 512], P(None, 'head'), may hold values from -0.078125 to 0.078125
- v_weight: bfloat16 [5120, 512], P(None, 'head'), may hold values from -0.078125 to 0.078125
- q_gain: float32 [128], replicated, may hold values from 1.2 to 13.2
- k_gain: float32 [128], replicated, may hold values from 1.2 to 13.2
Outputs:
- ctx_out: bfloat16 [32768, 2560], P('seq', 'head')
- fin_out: bfloat16 [1024, 2560], P('seq', 'head')
Inputs may be any that keep to these rules, and one draw needn't show every extreme that they name: lengths[b] counts the live rows at the start of context block b; the rest of the block is padding; the blocks hold 24576 live tokens together.
All inputs are finite; a program needn't handle non-finite values.
Results may differ from a plain program's by a relative error of at most 0.012.
The roundings to bfloat16 on the way count: a program that leaves them out, or rounds other values in their place, can miss the bound.
Values may be sent and summed in bfloat16 or wider, within the bound.
No kernel may reach another device: no remote copies, remote signals or barrier semaphores. Data moves between devices by JAX's collectives and lax.ppermute only.
A program may use at most 192 MiB of HBM per device.

v0:
```python
import functools

import jax
import jax.numpy as jnp
from jax import lax
from jax.experimental import pallas as pl
from jax.experimental.pallas import tpu as pltpu
from jax.sharding import PartitionSpec as P

HD = 128
GROUP = 5
KVH = 2
QH = 10
eps_norm = 1e-06
rope_base = 1000000.0
masked_score = -1e30
log2e = 1.4426950408889634
score_factor = HD ** (-0.5) * log2e
CHUNK = 128
F32 = jnp.float32
BF = jnp.bfloat16
NT = (((1,), (1,)), ((), ()))
SWAP = [(0, 1), (1, 0)]


def number(l, x, z, c):
    return ((l * 4 + x) * 4 + z) * 2 + c


def coords(s):
    return s // 32, s // 8 % 4, s // 2 % 4, s % 2


def route(move):
    return [(s, number(*move(*coords(s)))) for s in range(64)]


def to_z(k):
    return route(lambda l, x, z, c: (l, x, z ^ k, c))


def to_x(k):
    return route(lambda l, x, z, c: (l, x ^ k, z, c))


def both(move):
    pairs = []
    for s in range(64):
        l, x, z, c = coords(s)
        for h in range(2):
            to_l, to_h = move(l, h)
            pairs.append((2 * s + h, 2 * number(to_l, x, z, c) + to_h))
    return pairs


TO_CROSS = both(lambda l, h: (1 - l, 1 - h))
SWAP_FIRST = [(0, 1), (1, 0)]
SWAP_REST = [pair for pair in both(lambda l, h: (l, 1 - h)) if pair[0] > 1]
TO_Y = route(lambda l, x, z, c: (1 - l, x, z, c))
TO_CORE = route(lambda l, x, z, c: (l, x, z, 1 - c))


VMEM = pl.BlockSpec(memory_space=pltpu.VMEM)
SMEM = pl.BlockSpec(memory_space=pltpu.SMEM)
ANY = pl.BlockSpec(memory_space=pl.ANY)
WIDTH = (QH + 1) * HD


def cost(time):
    return pl.CostEstimate(
        flops=int(time * 1.15e9), bytes_accessed=int(time * 1e6), transcendentals=0
    )


def params(megabytes):
    return pltpu.CompilerParams(vmem_limit_bytes=megabytes << 20)


def normalize(own, others, gain_own, gain_other, place, normed, to, rows):
    half = own.shape[1]
    mine = pl.multiple_of(place[0] * half, half)
    theirs = pl.multiple_of((1 - place[0]) * half, half)

    def run(other):
        @pl.loop(0, rows // 16)
        def _(step):
            at = pl.ds(pl.multiple_of(step * 16, 16), 16)
            put = pl.ds(pl.multiple_of(step * 16 + to, 16), 16)
            a = own[at, :].astype(F32)
            b = other[at, :].astype(F32)
            total = jnp.sum(a * a + b * b, axis=1, keepdims=True)
            scale = lax.rsqrt(total / (2 * half) + eps_norm)
            normed[put, pl.ds(mine, half)] = (a * scale * gain_own[...]).astype(BF)
            normed[put, pl.ds(theirs, half)] = (b * scale * gain_other[...]).astype(BF)

    for use, other in others:
        if use is None:
            run(other)
        else:
            pl.when(use)(functools.partial(run, other))


def fin_project_kernel(
    place, own, other, near_own, near_other, gain_own, gain_other, q_gain, k_gain, cos, sin, wq, wk, wv,
    out, normed, weights, sems,
):
    copies = []
    for n in range(7):
        source = wq.at[:, pl.ds(n * 256, 256)] if n < 5 else (wk if n == 5 else wv)
        copies.append(pltpu.make_async_copy(source, weights.at[n], sems.at[n]))
        copies[-1].start()
    rows = own.shape[0]
    normalize(own, [(None, other)], gain_own, gain_other, place, normed, 0, rows)
    normalize(near_own, [(None, near_other)], gain_own, gain_other, place, normed, rows, rows)
    for n in range(7):
        copies[n].wait()
        gain = q_gain if n < 5 else k_gain
        project_columns(n, normed[...], weights[n], gain, cos, sin, out, out, QH * HD)


def fin_project(shared, turn, arrays):
    place, gain_own, gain_other, q_gain, k_gain, *weights = shared
    rows = 2 * arrays[0].shape[0]
    return pl.pallas_call(
        fin_project_kernel,
        out_shape=jax.ShapeDtypeStruct((rows, (QH + 2 * KVH) * HD), BF),
        in_specs=[SMEM] + [VMEM] * 10 + [ANY] * 3,
        out_specs=VMEM,
        scratch_shapes=[
            pltpu.VMEM((rows, 5120), BF),
            pltpu.VMEM((7, 5120, 256), BF),
            pltpu.SemaphoreType.DMA((7,)),
        ],
        compiler_params=params(52),
        cost_estimate=cost(0.1),
    )(place, *arrays, gain_own, gain_other, q_gain, k_gain, *turn, *weights)


def kv_kernel(
    count, place, gain_own, gain_other, k_gain, own, *rest,
):
    others, (cos, sin, wk, wv, kv_out, normed, weights, sems) = rest[:count], rest[count:]
    copies = [pltpu.make_async_copy(w, weights.at[i], sems.at[i]) for i, w in enumerate((wk, wv))]

    @pl.when(pl.program_id(0) == 0)
    def _():
        for copy in copies:
            copy.start()

    uses = [(None, others[0])]
    if count == 2:
        uses = [(place[1] != 0, others[0]), (place[1] == 0, others[1])]
    normalize(own, uses, gain_own, gain_other, place, normed, 0, own.shape[0])

    @pl.when(pl.program_id(0) == 0)
    def _():
        for copy in copies:
            copy.wait()

    for i in range(2):
        project_columns(5 + i, normed[...], weights[i], k_gain, cos, sin, None, kv_out, 0)


def kv_project(shared, turn, own, others, first, rows, room=40):
    place, gain_own, gain_other, _, k_gain, _, wk, wv = shared
    half = own.shape[1]
    tile = 128
    whole = lambda array: pl.BlockSpec(array.shape, lambda i: (0, 0))
    tiles = lambda width: pl.BlockSpec((tile, width), lambda i: (i, 0))
    from_row = lambda start, width: pl.BlockSpec((tile, width), lambda i: (i + start // tile, 0))
    later = functools.partial(from_row, first)
    return pl.pallas_call(
        functools.partial(kv_kernel, len(others)),
        grid=(rows // tile,),
        out_shape=(
            jax.ShapeDtypeStruct((rows, 2 * KVH * HD), BF),
            jax.ShapeDtypeStruct((rows, 2 * half), BF),
        ),
        in_specs=[SMEM, whole(gain_own), whole(gain_other), whole(k_gain)]
        + [later(half)] + [from_row(start, half) for _, start in others] + [later(HD)] * 2 + [ANY] * 2,
        out_specs=(tiles(2 * KVH * HD), tiles(2 * half)),
        scratch_shapes=[pltpu.VMEM((2, 2 * half, 256), BF), pltpu.SemaphoreType.DMA((2,))],
        compiler_params=params(room),
        cost_estimate=cost(0.02 * rows / 128),
    )(place, gain_own, gain_other, k_gain, own, *[array for array, _ in others], *turn, wk, wv)


def project_columns(n, normed, weight, gain, cos, sin, q_out, kv_out, shift):
    raw = jnp.dot(normed, weight, preferred_element_type=F32)
    for part in range(2):
        piece = raw[:, part * HD:(part + 1) * HD]
        if n == 6:
            kv_out[:, shift + (KVH + part) * HD:shift + (KVH + part + 1) * HD] = piece.astype(BF)
            continue
        mean = jnp.sum(piece * piece, axis=1, keepdims=True) * (1.0 / HD)
        piece = piece * lax.rsqrt(mean + eps_norm) * gain[...]
        turned = pltpu.roll(piece, HD // 2, 1)
        piece = (piece * cos[...] + turned * sin[...]).astype(BF)
        if n < 5:
            q_out[:, n * 256 + part * HD:n * 256 + (part + 1) * HD] = piece
        else:
            kv_out[:, shift + part * HD:shift + (part + 1) * HD] = piece


def queries_kernel(q_gain, cos, sin, wq, normed, out):
    project_columns(0, normed[...], wq[...], q_gain, cos, sin, out, None, 0)


def project_queries(shared, turn, normed, first, time=8):
    q_gain, wq = shared[3], shared[5]
    rows, depth = normed.shape
    whole = lambda array: pl.BlockSpec(array.shape, lambda i: (0, 0))
    turned = pl.BlockSpec((rows, HD), lambda i: (first // rows, 0))
    return pl.pallas_call(
        queries_kernel,
        grid=(5,),
        out_shape=jax.ShapeDtypeStruct((rows, QH * HD), BF),
        in_specs=[whole(q_gain), turned, turned, pl.BlockSpec((depth, 256), lambda i: (0, i)), whole(normed)],
        out_specs=pl.BlockSpec((rows, 256), lambda i: (0, i)),
        compiler_params=params(40),
        cost_estimate=cost(time),
    )(q_gain, *turn, wq, normed)


def guard(kv, count, keys, values):
    rows = kv.shape[0]
    live = lax.broadcasted_iota(jnp.int32, (rows, HD), 0) < count
    ones = jnp.where(live, 1.0, 0.0).astype(BF)
    for g in range(KVH):
        key = kv[:, g * HD:(g + 1) * HD].astype(F32)
        keys[:, g * HD:(g + 1) * HD] = jnp.where(live, key, key[0:1, :]).astype(BF)
        value = kv[:, (KVH + g) * HD:(KVH + g + 1) * HD].astype(F32)
        values[:, 2 * g * HD:(2 * g + 1) * HD] = jnp.where(live, value, 0.0).astype(BF)
        values[:, (2 * g + 1) * HD:(2 * g + 2) * HD] = ones


def ctx_kernel(first, info, anchor, q, kv, *refs):
    out, keys, values, own_keys, own_values = refs[-5:]
    position, own_length, anchor_length = info[0], info[1], info[2]
    guard(anchor, jnp.where(position > 0, anchor_length, 0), keys, values)
    own_keys[...] = kv[:, :KVH * HD]
    for g in range(KVH):
        own_values[:, 2 * g * HD:(2 * g + 1) * HD] = kv[:, (KVH + g) * HD:(KVH + g + 1) * HD]
        own_values[:, (2 * g + 1) * HD:(2 * g + 2) * HD] = jnp.ones((kv.shape[0], HD), BF)
    tile = 128
    row = lax.broadcasted_iota(jnp.int32, (tile, HD), 0)
    causal = lax.broadcasted_iota(jnp.int32, (tile, tile), 1) <= lax.broadcasted_iota(
        jnp.int32, (tile, tile), 0
    )
    for start in range(0, out.shape[0], tile):
        before = first + start
        at = put = slice(start, start + tile)
        live = row + before < own_length
        for h in range(QH):
            g = h // GROUP
            here, there = slice(h * HD, (h + 1) * HD), slice(g * HD, (g + 1) * HD)
            both_columns = slice(2 * g * HD, (2 * g + 2) * HD)
            query = q[at, here]
            scores = [lax.dot_general(query, keys[:, there], NT, preferred_element_type=F32)]
            if before:
                scores.append(
                    lax.dot_general(query, own_keys[:before, there], NT, preferred_element_type=F32)
                )
            last = lax.dot_general(
                query, own_keys[before:before + tile, there], NT, preferred_element_type=F32
            )
            scores.append(jnp.where(causal, last, masked_score))
            peak = functools.reduce(
                jnp.maximum, [jnp.max(score, axis=1, keepdims=True) for score in scores]
            ) * score_factor
            p = [jnp.exp2(score * score_factor - peak).astype(BF) for score in scores]
            mixed = jnp.dot(p[0], values[:, both_columns], preferred_element_type=F32)
            if before:
                mixed += jnp.dot(p[1], own_values[:before, both_columns], preferred_element_type=F32)
            mixed += jnp.dot(
                p[-1], own_values[before:before + tile, both_columns], preferred_element_type=F32
            )
            result = mixed[:, :HD] / mixed[:, HD:]
            out[put, here] = jnp.where(live, result, 0.0).astype(BF)


def ctx_attention(first, rows, info, q, anchor, kv, base):
    count = kv.shape[0]
    extra = [] if base is None else [base]
    return pl.pallas_call(
        functools.partial(ctx_kernel, first),
        grid=(1,),
        out_shape=jax.ShapeDtypeStruct((count, QH * HD), BF),
        in_specs=[SMEM] + [VMEM] * 3 + [pl.BlockSpec(memory_space=pl.ANY)] * len(extra),
        out_specs=pl.BlockSpec((rows, QH * HD), lambda i: (first // rows, 0)),
        scratch_shapes=[
            pltpu.VMEM((count, KVH * HD), BF),
            pltpu.VMEM((count, 2 * KVH * HD), BF),
            pltpu.VMEM((count, KVH * HD), BF),
            pltpu.VMEM((count, 2 * KVH * HD), BF),
        ],
        input_output_aliases={4: 0} if extra else {},
        compiler_params=params(10),
        cost_estimate=cost(5),
    )(info, anchor, q, kv, *extra)


def store_stats(out, at, peaks, totals):
    lane = lax.broadcasted_iota(jnp.int32, (at.stop - at.start, HD), 1)
    peak, total = jnp.zeros(lane.shape, F32), jnp.zeros(lane.shape, F32)
    for h in range(QH):
        peak = jnp.where(lane == h, peaks[h], peak)
        total = jnp.where(lane == h, totals[h], total)
    high = total.astype(BF).astype(F32)
    stats = peak + pltpu.roll(high, 16, 1) + pltpu.roll(total - high, 32, 1)
    out[at, QH * HD:] = stats.astype(BF)


def fin_kernel(first, count, info, q, *refs):
    kvs = refs[:count]
    out, keys, values, joined = refs[count:]
    own_length = info[1]
    to = 0
    for kv in kvs:
        joined[to:to + kv.shape[0], :] = kv[...]
        to += kv.shape[0]
    guard(joined, own_length - first, keys, values)
    floor = jnp.where(own_length > first, 0.0, masked_score)
    tile = 256
    for start in range(0, q.shape[0], tile):
        at = slice(start, start + tile)
        peaks, totals = [], []
        for h in range(QH):
            g = h // GROUP
            here, there = slice(h * HD, (h + 1) * HD), slice(g * HD, (g + 1) * HD)
            score = lax.dot_general(q[at, here], keys[:, there], NT, preferred_element_type=F32)
            peak = (jnp.max(score, axis=1, keepdims=True) * score_factor).astype(BF).astype(F32)
            p = jnp.exp2(score * score_factor - peak).astype(BF)
            mixed = jnp.dot(p, values[:, 2 * g * HD:(2 * g + 2) * HD], preferred_element_type=F32)
            out[at, here] = mixed[:, :HD].astype(BF)
            peaks.append(peak + floor)
            totals.append(mixed[:, HD:])
        store_stats(out, at, peaks, totals)


def fin_attention(first, info, q, kvs):
    rows, keys = q.shape[0], sum(kv.shape[0] for kv in kvs)
    return pl.pallas_call(
        functools.partial(fin_kernel, first, len(kvs)),
        out_shape=jax.ShapeDtypeStruct((rows, WIDTH), BF),
        in_specs=[SMEM] + [VMEM] * (1 + len(kvs)),
        out_specs=VMEM,
        scratch_shapes=[
            pltpu.VMEM((keys, KVH * HD), BF),
            pltpu.VMEM((keys, 2 * KVH * HD), BF),
            pltpu.VMEM((keys, 2 * KVH * HD), BF),
        ],
        compiler_params=params(10),
        cost_estimate=cost(5),
    )(info, q, *kvs)


def self_kernel(info, ids, q, kv, kv_across, out):
    rows = out.shape[0]
    shift = QH * HD
    tall = GROUP * rows
    queries = info[0] * rows + lax.rem(lax.broadcasted_iota(jnp.int32, (tall, 512), 0), rows)
    allowed = [ids[:, :512] <= queries, ids[:, 512:] <= queries]
    peaks, totals = [], []
    for g in range(KVH):
        heads = range(g * GROUP, (g + 1) * GROUP)
        query = jnp.concatenate([q[:rows, h * HD:(h + 1) * HD] for h in heads], axis=0)
        there = slice(shift + g * HD, shift + (g + 1) * HD)
        value = slice(shift + (KVH + g) * HD, shift + (KVH + g + 1) * HD)
        scores = [
            jnp.where(
                mask, lax.dot_general(query, part[:, there], NT, preferred_element_type=F32), masked_score
            )
            for mask, part in zip(allowed, (kv, kv_across))
        ]
        peak = jnp.maximum(*[jnp.max(score, axis=1, keepdims=True) for score in scores])
        peak = (peak * score_factor).astype(BF).astype(F32)
        p = [jnp.exp2(score * score_factor - peak) for score in scores]
        mixed = sum(
            jnp.dot(weight.astype(BF), part[:, value], preferred_element_type=F32)
            for weight, part in zip(p, (kv, kv_across))
        )
        total = sum(jnp.sum(weight, axis=1, keepdims=True) for weight in p)
        for i, h in enumerate(heads):
            at = slice(i * rows, (i + 1) * rows)
            out[:, h * HD:(h + 1) * HD] = mixed[at].astype(BF)
            peaks.append(peak[at])
            totals.append(total[at])
    store_stats(out, slice(0, rows), peaks, totals)


def self_attention(info, ids, q, kv, kv_across, rows):
    return pl.pallas_call(
        self_kernel,
        out_shape=jax.ShapeDtypeStruct((rows, WIDTH), BF),
        in_specs=[SMEM] + [VMEM] * 4,
        out_specs=VMEM,
        compiler_params=params(10),
        cost_estimate=cost(5),
    )(info, ids, q, kv, kv_across)


def merge_kernel(count, final, info, *refs):
    parts, outs = refs[:count], refs[count:]
    rows = outs[0].shape[0]
    tile = min(rows, 64)
    lane = lax.broadcasted_iota(jnp.int32, (tile, HD), 1)
    for k, out in enumerate(outs):
        for start in range(0, rows, tile):
            if len(outs) == 4:
                first = pl.multiple_of(lax.rem(info[0] + k, 4) * rows, rows) + start
                at = pl.ds(pl.multiple_of(first, min(tile, 16)), tile)
            else:
                at = slice(k * rows + start, k * rows + start + tile)
            to = slice(start, start + tile)
            stats = [part[at, QH * HD:].astype(F32) for part in parts]
            top = functools.reduce(jnp.maximum, stats)
            weights = [jnp.exp2(jnp.where(lane < QH, stat - top, 0.0)) for stat in stats]
            totals = [pltpu.roll(stat, HD - 16, 1) + pltpu.roll(stat, HD - 32, 1) for stat in stats]
            total = sum(w * t for w, t in zip(weights, totals))
            if final:
                inverse = 1.0 / jnp.where(lane < QH, total, 1.0)
                weights = [w * inverse for w in weights]
            for h in range(QH):
                here = slice(h * HD, (h + 1) * HD)
                mixed = sum(
                    part[at, here].astype(F32) * w[:, h:h + 1] for part, w in zip(parts, weights)
                )
                out[to, here] = mixed.astype(BF)
            if not final:
                total = jnp.where(lane < QH, total, 0.0)
                top = jnp.where(lane < QH, top, 0.0)
                high = total.astype(BF).astype(F32)
                packed = top + pltpu.roll(high, 16, 1) + pltpu.roll(total - high, 32, 1)
                out[to, QH * HD:] = packed.astype(BF)


def merge(parts, count=1, turn=None, final=False):
    rows = parts[0].shape[0] // count
    turn = jnp.zeros((1,), jnp.int32) if turn is None else turn.reshape(1)
    shape = jax.ShapeDtypeStruct((rows, QH * HD if final else WIDTH), BF)
    return pl.pallas_call(
        functools.partial(merge_kernel, len(parts), final),
        out_shape=(shape,) * count,
        in_specs=[SMEM] + [VMEM] * len(parts),
        out_specs=(VMEM,) * count,
        compiler_params=params(10),
        cost_estimate=cost(0.3 * sum(part.shape[0] for part in parts) / 128),
    )(turn, *parts)


def join_kernel(*refs):
    to = 0
    for ref in refs[:-1]:
        refs[-1][to:to + ref.shape[0], :] = ref[...]
        to += ref.shape[0]


def join(*arrays):
    return pl.pallas_call(
        join_kernel,
        out_shape=jax.ShapeDtypeStruct((sum(a.shape[0] for a in arrays), arrays[0].shape[1]), BF),
        in_specs=[VMEM] * len(arrays),
        out_specs=VMEM,
        compiler_params=params(10),
        cost_estimate=cost(0.02),
    )(*arrays)


def send_on(arrays, to):
    return [lax.ppermute(array, "seq", to(k)) for k, array in enumerate(arrays) if k]


def broadcast_stages(seq):
    l, x, z, c = coords(seq)
    return [
        (route_from(lambda l, x, z, c: (l, x, z, c) == (0, 0, 0, 0), lambda l, x, z, c: (l, x, 2, c)),
         (l == 0) & (x == 0) & (z == 2) & (c == 0)),
        (route_from(lambda l, x, z, c: l == 0 and x == 0 and z in (0, 2) and c == 0, lambda l, x, z, c: (l, x, z + 1, c)),
         (l == 0) & (x == 0) & (z % 2 == 1) & (c == 0)),
        (route_from(lambda l, x, z, c: l == 0 and x == 0 and c == 0, lambda l, x, z, c: (l, 2, z, c)),
         (l == 0) & (x == 2) & (c == 0)),
        (route_from(lambda l, x, z, c: l == 0 and x in (0, 2) and c == 0, lambda l, x, z, c: (l, x + 1, z, c)),
         (l == 0) & (x % 2 == 1) & (c == 0)),
        (route_from(lambda l, x, z, c: l == 0 and c == 0, lambda l, x, z, c: (1, x, z, c)),
         (l == 1) & (c == 0)),
        (route_from(lambda l, x, z, c: c == 0, lambda l, x, z, c: (l, x, z, 1)), c == 1),
    ]


def route_from(holds, move):
    return [(s, number(*move(*coords(s)))) for s in range(64) if holds(*coords(s))]


def turns(positions):
    exponent = jnp.arange(HD // 2, dtype=F32) * (-2.0 / HD)
    frequency = jnp.power(F32(rope_base), exponent)
    angles = positions.astype(F32)[:, None] * frequency[None, :]
    cos, sin = jnp.cos(angles), jnp.sin(angles)
    return jnp.concatenate([cos, cos], axis=1), jnp.concatenate([-sin, sin], axis=1)


def tie(*values):
    return lax.optimization_barrier(values)


def local(ctx_hidden, fin_hidden, lengths, ln_gain, q_weight, k_weight, v_weight, q_gain, k_gain):
    ctx_count, half = ctx_hidden.shape
    fin_count = fin_hidden.shape[0]
    head = lax.axis_index("head").astype(jnp.int32)
    seq = lax.axis_index("seq").astype(jnp.int32)
    axes = ("seq", "head")
    own_gain = ln_gain.reshape(1, half)
    high = lax.reduce_precision(own_gain, 8, 7)
    middle = lax.reduce_precision(own_gain - high, 8, 7)
    low = own_gain - high - middle
    pieces = [piece.astype(BF) for piece in (high, middle, low)]
    sent = jnp.concatenate([fin_hidden] + pieces + [jnp.zeros((13, half), BF)], axis=0)
    received = lax.ppermute(sent, "head", SWAP)
    near_own = lax.ppermute(fin_hidden, "seq", TO_Y)
    near_other = lax.ppermute(fin_hidden, axes, TO_CROSS)
    split = ctx_count // 2
    soon = lax.ppermute(ctx_hidden[:split], "head", SWAP)
    ahead = lax.ppermute(ctx_hidden[split:], axes, SWAP_FIRST)
    others = lax.ppermute(ctx_hidden[split:], axes, SWAP_REST)

    weights = (q_weight, k_weight, v_weight)
    block_ids = jnp.arange(64, dtype=jnp.int32)
    own_start = jnp.sum(jnp.where(block_ids < seq, lengths, 0))
    own_length = jnp.sum(jnp.where(block_ids == seq, lengths, 0))
    live_total = jnp.sum(lengths)
    my_l, my_x, my_z, my_c = coords(seq)
    near = number(1 - my_l, my_x, my_z, my_c)
    fin_ids = jnp.arange(fin_count, dtype=jnp.int32)
    fin_positions = live_total + jnp.concatenate([seq * fin_count + fin_ids, near * fin_count + fin_ids])

    info = jnp.stack([seq, own_length, lengths[0], jnp.int32(fin_count)])
    other_gain = sum(received[fin_count + i:fin_count + i + 1].astype(F32) for i in range(3))
    shared = (
        jnp.stack([head, seq]), own_gain, other_gain, q_gain.reshape(1, HD), k_gain.reshape(1, HD), *weights,
    )
    own_qkv = fin_project(shared, turns(fin_positions), (fin_hidden, received, near_own, near_other))
    own_qkv, own_start = tie(own_qkv, own_start)
    turn = turns(own_start + jnp.arange(ctx_count, dtype=jnp.int32))
    def double(array, pairs):
        return lax.ppermute(array, "seq", pairs)

    passed = double(own_qkv, to_x(1))
    own_qkv, passed, turn = tie(own_qkv, passed, turn)
    gathered = join(own_qkv, passed)
    gathered = join(gathered, double(gathered, to_x(2)))
    passed = double(gathered, to_z(1))
    gathered, soon = tie(gathered, soon)
    kv_soon, normed = kv_project(shared, turn, ctx_hidden, ((soon, 0),), 0, split)
    passed, kv_soon = tie(passed, kv_soon)
    gathered = join(gathered, passed)
    passed = double(gathered, to_z(2))
    kv_soon, ahead = tie(kv_soon, ahead)
    kv_ahead = kv_project(shared, turn, ctx_hidden, ((ahead, 0),), split, split)[0]
    stages = broadcast_stages(seq)
    anchor = join(kv_soon, kv_ahead)

    def send(stage):
        return lax.ppermute(anchor, "seq", stages[stage][0])

    def take(stage):
        return jnp.where(stages[stage][1], arrived, anchor)

    arrived = send(0)
    anchor, normed = tie(anchor, normed)
    q_soon = project_queries(shared, turn, normed, 0, 0.1)
    q_soon, arrived, others, passed = tie(q_soon, arrived, others, passed)
    anchor = take(0)
    arrived = send(1)
    gathered = join(gathered, passed)
    across = lax.ppermute(gathered, "seq", TO_CORE)
    kv_late, normed = kv_project(
        shared, turn, ctx_hidden, ((others, 0), (ahead, 0)), split, split, room=58
    )
    kv_late, arrived, across = tie(kv_late, arrived, across)
    anchor = take(1)
    arrived = send(2)
    kv = join(kv_soon, kv_late)
    away = fin_attention(0, info, across, [kv])
    passed = lax.ppermute(away, "seq", TO_CORE)
    part = fin_attention(0, info, gathered, [kv])
    part, passed, normed = tie(part, passed, normed)
    partial = merge([part, passed], 4)
    passed = send_on(partial, to_z)
    partial, normed, arrived = tie(partial, normed, arrived)
    anchor = take(2)
    arrived = send(3)
    q_late = project_queries(shared, turn, normed, split)
    q_late, arrived = tie(q_late, arrived)
    anchor = take(3)
    arrived = send(4)
    slot = jnp.arange(64, dtype=jnp.int32)
    owner = number(my_l ^ (slot % 2), my_x ^ (slot // 2 % 4), my_z ^ (slot // 8 % 4), my_c ^ (slot // 32))
    ids = (owner[:, None] * fin_count + fin_ids[None, :]).reshape(1, -1)
    own_part = self_attention(info, ids, own_qkv, gathered, across, fin_count)
    passed, own_part, arrived = tie(passed, own_part, arrived)
    anchor = take(4)
    partial = merge([partial[0]] + passed, 4)
    passed = send_on(partial, to_x)
    partial, anchor = tie(partial, anchor)
    arrived = send(5)
    anchor = take(5)
    ctx_out = ctx_attention(0, split, info, q_soon, anchor, kv, None)
    passed, ctx_out = tie(passed, ctx_out)
    partial = merge([partial[0]] + passed, 2)
    passed = lax.ppermute(partial[1], "seq", TO_Y)
    partial, ctx_out = tie(partial, ctx_out)
    ctx_out = ctx_attention(split, split, info, q_late, anchor, kv, ctx_out)
    passed, ctx_out = tie(passed, ctx_out)
    fin_out = merge([partial[0], passed, own_part], final=True)[0]
    return ctx_out, fin_out


def solution(mesh):
    return jax.shard_map(
        local,
        mesh=mesh,
        in_specs=(
            P("seq", "head"),
            P("seq", "head"),
            P(),
            P("head"),
            P(None, "head"),
            P(None, "head"),
            P(None, "head"),
            P(),
            P(),
        ),
        out_specs=(P("seq", "head"), P("seq", "head")),
        check_vma=False,
    )
```

profile of v0, /device:TPU:16, one launch (start us, length us, event | category | flops | bytes accessed | tf_op | source)
XLA Modules:
  0.0 160.5 jit_solution(3500591323848232750)
XLA Ops:
  0.6 1.4 collective-permute-start.1
  2.0 0.7 fusion.1
  2.8 1.2 concatenate.22
  4.0 2.9 %collective-permute-start = (bf16[32,2560]{1,0:T(8,128)(2,1)S(1)}, bf16[32,2560]{1,0:T(8,128)(2,1)S(1)}, u32[]{:S(2)}, u32[]{:S(2)}) collective-permute-start(bf16[32,2560]{1,0:T(8,128)(2,1)S(1)} %concatenate.22), channel_id=1, source_target_pairs={{0,1},{1,0},{2,3},{3,2},{4,5},{5,4},{6,7},{7,6},{8,9},{9,8},{10,11... | collective-permute-start | bytes 491528 | tf_op jit(solution)/shard_map/ppermute | solution.py:519
  6.9 3.4 %fusion.20 = (bf16[256,2560]{1,0:T(8,128)(2,1)}, bf16[256,2560]{1,0:T(8,128)(2,1)}) fusion(bf16[512,2560]{1,0:T(8,128)(2,1)} %own.7), kind=kLoop, calls=%fused_computation.67 | loop fusion | bytes 5242880 | tf_op jit(solution)/shard_map/slice | solution.py:524
  10.3 0.7 collective-permute-start.5
  11.0 4.7 %collective-permute-start.7 = (bf16[256,2560]{1,0:T(8,128)(2,1)}, bf16[256,2560]{1,0:T(8,128)(2,1)}, u32[]{:S(2)}, u32[]{:S(2)}) collective-permute-start(bf16[256,2560]{1,0:T(8,128)(2,1)} %get-tuple-element.123), channel_id=1, source_target_pairs={{0,1},{1,0}} | collective-permute-start | bytes 3932168 | tf_op jit(solution)/shard_map/ppermute | solution.py:524
  15.9 0.7 fusion.7
  16.6 0.7 fusion.18
  17.8 9.1 %shard_map.104.refs_0_.q = bf16[32,1792]{1,0:T(8,128)(2,1)S(1)} custom-call(s32[2]{0:T(128)S(1)} %pad_add_fusion.1.place, bf16[16,2560]{1,0:T(8,128)(2,1)S(1)} %copy-done.9, bf16[32,2560]{1,0:T(8,128)(2,1)S(1)} %collective-permute-done.other, bf16[16,2560]{1,0:T(8,128)(2,1)S(1)} %collective-permute-done.1.near_own, ...), custom_call_target="tpu_custom_call" | custom-call | flops 115000000 | bytes 100000 | tf_op jit(solution)/shard_map/pallas_call | solution.py:124
  27.7 1.0 fusion
  29.0 3.3 %collective-permute-done.3.refs_1_ = bf16[32,1792]{1,0:T(8,128)(2,1)S(1)} collective-permute-done((bf16[32,1792]{1,0:T(8,128)(2,1)S(1)}, bf16[32,1792]{1,0:T(8,128)(2,1)S(1)}, u32[]{:S(2)}, u32[]{:S(2)}) %collective-permute-start.3) | collective-permute-done | bytes 114720 | tf_op jit(solution)/shard_map/ppermute | solution.py:546
  32.5 7.5 %collective-permute-done.4.refs_1_ = bf16[64,1792]{1,0:T(8,128)(2,1)S(1)} collective-permute-done((bf16[64,1792]{1,0:T(8,128)(2,1)S(1)}, bf16[64,1792]{1,0:T(8,128)(2,1)S(1)}, u32[]{:S(2)}, u32[]{:S(2)}) %collective-permute-start.4) | collective-permute-done | bytes 229408 | tf_op jit(solution)/shard_map/ppermute | solution.py:546
  40.1 0.7 collective-permute-start.9
  40.9 1.1 collective-permute-done.5.rest_0_
  42.0 5.9 %shard_map.107 = (bf16[256,512]{1,0:T(8,128)(2,1)S(1)}, bf16[256,5120]{1,0:T(8,128)(2,1)S(1)}) custom-call(s32[2]{0:T(128)S(1)} %pad_add_fusion.1.place, f32[1,2560]{1,0:T(1,128)S(1)} %reshape.137.gain_own, f32[1,2560]{1,0:T(1,128)S(1)} %fusion.2.gain_other, f32[1,128]{1,0:T(1,128)S(1)} %bitcast.8, bf16[512,2560]{1,0:T(8,128)(2,1)S(1)} %copy-done, ...), custom_call_target="tpu_custom_call" | custom-call | flops 46000000 | bytes 40000 | tf_op jit(solution)/shard_map/pallas_call | solution.py:172
  47.9 0.7 collective-permute-done.6.refs_1_
  48.7 4.1 %collective-permute-start.10 = (bf16[256,1792]{1,0:T(8,128)(2,1)S(1)}, bf16[256,1792]{1,0:T(8,128)(2,1)S(1)}, u32[]{:S(2)}, u32[]{:S(2)}) collective-permute-start(bf16[256,1792]{1,0:T(8,128)(2,1)S(1)} %shard_map.108.refs_0_), channel_id=1, source_target_pairs={{0,8},{2,10},{4,12},{6,14},{8,0},{10,2},{12,4},{14,6},{16,24},{18,... | collective-permute-start | bytes 2752520 | tf_op jit(solution)/shard_map/ppermute | solution.py:546
  52.8 17.1 %collective-permute-done.7.rest_0_.rest_1_ = bf16[256,2560]{1,0:T(8,128)(2,1)} collective-permute-done((bf16[256,2560]{1,0:T(8,128)(2,1)}, bf16[256,2560]{1,0:T(8,128)(2,1)}, u32[]{:S(2)}, u32[]{:S(2)}) %collective-permute-start.7) | collective-permute-done | bytes 1310752 | tf_op jit(solution)/shard_map/ppermute | solution.py:524
  69.9 5.9 %shard_map.109 = (bf16[256,512]{1,0:T(8,128)(2,1)S(1)}, bf16[256,5120]{1,0:T(8,128)(2,1)}) custom-call(s32[2]{0:T(128)S(1)} %pad_add_fusion.1.place, f32[1,2560]{1,0:T(1,128)S(1)} %reshape.137.gain_own, f32[1,2560]{1,0:T(1,128)S(1)} %fusion.2.gain_other, f32[1,128]{1,0:T(1,128)S(1)} %bitcast.9, bf16[512,2560]{1,0:T(8,128)(2,1)S(1)} %copy-done, ...), custom_call_target="tpu_custom_call" | custom-call | flops 46000000 | bytes 40000 | tf_op jit(solution)/shard_map/pallas_call | solution.py:172
  75.9 1.3 collective-permute-start.8
  77.2 8.3 %shard_map.111.q = bf16[256,1280]{1,0:T(8,128)(2,1)S(1)} custom-call(f32[1,128]{1,0:T(1,128)S(1)} %bitcast.11, f32[512,128]{1,0:T(8,128)S(1)} %pad_maximum_fusion.rest_1_.cos.rest_2_, f32[512,128]{1,0:T(8,128)S(1)} %pad_maximum_fusion.1.rest_2_.sin.rest_3_, bf16[5120,1280]{1,0:T(8,128)(2,1)} %wq.5, bf16[256,5120]{1,0:T(8,128)(2,1)S(1)} %get-tuple-element.76.normed), custom_call_target="tpu_custom_call" | custom-call | flops 115000000 | bytes 100000 | tf_op jit(solution)/shard_map/pallas_call | solution.py:214
  85.6 0.9 copy-done.27
  87.1 1.5 collective-permute-start.11
  88.6 0.7 pad_add_fusion.info
  89.3 8.2 %shard_map.113 = (bf16[256,512]{1,0:T(8,128)(2,1)}, bf16[256,5120]{1,0:T(8,128)(2,1)}) custom-call(s32[2]{0:T(128)} %copy-done.14, f32[1,2560]{1,0:T(1,128)} %copy-done.11, f32[1,2560]{1,0:T(1,128)} %copy-done.12, f32[1,128]{1,0:T(1,128)} %bitcast.6, bf16[512,2560]{1,0:T(8,128)(2,1)} %own.7, bf16[256,2560]{1,0:T(8,128)(2,1)} %copy-done.25, ...), custom_call_target="tpu_custom_call" | custom-call | flops 46000000 | bytes 40000 | tf_op jit(solution)/shard_map/pallas_call | solution.py:172
  97.6 1.1 copy-done.10
  98.8 6.3 %shard_map.116 = bf16[512,1408]{1,0:T(8,128)(2,1)} custom-call(s32[4]{0:T(128)S(1)} %pad_add_fusion.info, bf16[512,1792]{1,0:T(8,128)(2,1)} %collective-permute-done.12.q.kv_across, bf16[512,512]{1,0:T(8,128)(2,1)S(1)} %shard_map.114.refs_0_.kv), custom_call_target="tpu_custom_call" | custom-call | flops 5750000128 | bytes 5000000 | tf_op jit(solution)/shard_map/pallas_call | solution.py:343
  105.4 1.3 collective-permute-start.14
  106.7 4.2 %shard_map.115.refs_0_ = bf16[512,1408]{1,0:T(8,128)(2,1)S(1)} custom-call(s32[4]{0:T(128)S(1)} %pad_add_fusion.info, bf16[512,1792]{1,0:T(8,128)(2,1)S(1)} %shard_map.112.q.kv, bf16[512,512]{1,0:T(8,128)(2,1)S(1)} %shard_map.114.refs_0_.kv), custom_call_target="tpu_custom_call" | custom-call | flops 5750000128 | bytes 5000000 | tf_op jit(solution)/shard_map/pallas_call | solution.py:343
  110.9 4.1 %shard_map.117 = (bf16[128,1408]{1,0:T(8,128)(2,1)S(1)}, bf16[128,1408]{1,0:T(8,128)(2,1)S(1)}, bf16[128,1408]{1,0:T(8,128)(2,1)S(1)}, bf16[128,1408]{1,0:T(8,128)(2,1)S(1)}) custom-call(s32[1]{0:T(128)} %constant.135.clone.1.info, bf16[512,1408]{1,0:T(8,128)(2,1)S(1)} %shard_map.115.refs_0_, bf16[512,1408]{1,0:T(8,128)(2,1)} %collective-permute-done.13.refs_1_), custom_call_target="tpu_custom_call" | custom-call | flops 2760000000 | bytes 2400000 | tf_op jit(solution)/shard_map/pallas_call | solution.py:442
  115.1 1.1 collective-permute-start.15
  116.2 2.9 %collective-permute-start.16 = (bf16[128,1408]{1,0:T(8,128)(2,1)S(1)}, bf16[128,1408]{1,0:T(8,128)(2,1)S(1)}, u32[]{:S(2)}, u32[]{:S(2)}) collective-permute-start(bf16[128,1408]{1,0:T(8,128)(2,1)S(1)} %get-tuple-element.89), channel_id=1, source_target_pairs={{0,8},{2,10},{4,12},{6,14},{8,0},{10,2},{12,4},{14,6},{16,24},{18,... | collective-permute-start | bytes 1081352 | tf_op jit(solution)/shard_map/ppermute | solution.py:471
  119.1 0.8 collective-permute-start.17
  120.0 1.3 collective-permute-start.18
  121.3 8.3 %shard_map.119.q = bf16[256,1280]{1,0:T(8,128)(2,1)S(1)} custom-call(f32[1,128]{1,0:T(1,128)S(1)} %bitcast.12, f32[512,128]{1,0:T(8,128)S(1)} %copy-done.4, f32[512,128]{1,0:T(8,128)S(1)} %copy-done.6, bf16[5120,1280]{1,0:T(8,128)(2,1)} %wq.5, bf16[256,5120]{1,0:T(8,128)(2,1)S(1)} %copy-done.18), custom_call_target="tpu_custom_call" | custom-call | flops 9200000000 | bytes 8000000 | tf_op jit(solution)/shard_map/pallas_call | solution.py:214
  129.8 1.3 collective-permute-start.19
  131.1 2.3 %shard_map.118.refs_2_ = bf16[16,1408]{1,0:T(8,128)(2,1)S(1)} custom-call(s32[4]{0:T(128)S(1)} %pad_add_fusion.info, s32[1,1024]{1,0:T(1,128)S(1)} %add.184.ids, bf16[32,1792]{1,0:T(8,128)(2,1)S(1)} %shard_map.104.refs_0_.q, bf16[512,1792]{1,0:T(8,128)(2,1)S(1)} %shard_map.112.q.kv, bf16[512,1792]{1,0:T(8,128)(2,1)} %collective-permute-done.12.q.kv_across), custom_call_target="tpu_custom_call" | custom-call | flops 5750000128 | bytes 5000000 | tf_op jit(solution)/shard_map/pallas_call | solution.py:393
  133.4 1.0 collective-permute-done.16.refs_2_
  134.4 2.7 %collective-permute-done.17.refs_3_ = bf16[128,1408]{1,0:T(8,128)(2,1)S(1)} collective-permute-done((bf16[128,1408]{1,0:T(8,128)(2,1)S(1)}, bf16[128,1408]{1,0:T(8,128)(2,1)S(1)}, u32[]{:S(2)}, u32[]{:S(2)}) %collective-permute-start.17) | collective-permute-done | bytes 360480 | tf_op jit(solution)/shard_map/ppermute | solution.py:471
  137.8 1.2 shard_map.120
  139.0 1.5 collective-permute-start.23
  140.5 0.8 collective-permute-start.20
  141.3 4.0 %collective-permute-start.22 = (bf16[32,1408]{1,0:T(8,128)(2,1)S(1)}, bf16[32,1408]{1,0:T(8,128)(2,1)S(1)}, u32[]{:S(2)}, u32[]{:S(2)}) collective-permute-start(bf16[32,1408]{1,0:T(8,128)(2,1)S(1)} %get-tuple-element.103), channel_id=1, source_target_pairs={{0,48},{2,50},{4,52},{6,54},{8,56},{10,58},{12,60},{14,62},{16,32}... | collective-permute-start | bytes 270344 | tf_op jit(solution)/shard_map/ppermute | solution.py:471
  145.4 5.0 %shard_map.121.refs_0_ = bf16[512,1280]{1,0:T(8,128)(2,1)} custom-call(s32[4]{0:T(128)S(1)} %pad_add_fusion.info, bf16[512,512]{1,0:T(8,128)(2,1)S(1)} %broadcast_select_fusion.anchor, bf16[256,1280]{1,0:T(8,128)(2,1)S(1)} %copy-done.8, bf16[512,512]{1,0:T(8,128)(2,1)S(1)} %shard_map.114.refs_0_.kv), custom_call_target="tpu_custom_call" | custom-call | flops 5750000128 | bytes 5000000 | tf_op jit(solution)/shard_map/pallas_call | solution.py:285
  150.7 2.8 %collective-permute-start.24 = (bf16[16,1408]{1,0:T(8,128)(2,1)S(1)}, bf16[16,1408]{1,0:T(8,128)(2,1)S(1)}, u32[]{:S(2)}, u32[]{:S(2)}) collective-permute-start(bf16[16,1408]{1,0:T(8,128)(2,1)S(1)} %get-tuple-element.111), channel_id=1, source_target_pairs={{0,64},{2,66},{4,68},{6,70},{8,72},{10,74},{12,76},{14,78},{16,80}... | collective-permute-start | bytes 135176 | tf_op jit(solution)/shard_map/ppermute | solution.py:611
  153.5 6.2 %shard_map.123 = bf16[512,1280]{1,0:T(8,128)(2,1)} custom-call(s32[4]{0:T(128)S(1)} %pad_add_fusion.info, bf16[512,512]{1,0:T(8,128)(2,1)S(1)} %broadcast_select_fusion.anchor, bf16[256,1280]{1,0:T(8,128)(2,1)S(1)} %copy-done.22, bf16[512,512]{1,0:T(8,128)(2,1)S(1)} %shard_map.114.refs_0_.kv, ...), custom_call_target="tpu_custom_call", output_to_operand_aliasing={{}: (4, {})} | custom-call | flops 5750000128 | bytes 5000000 | tf_op jit(solution)/shard_map/pallas_call | solution.py:285
  159.6 0.9 shard_map.124
  (114 shorter events, 4.1 us)
Async XLA Ops:
  0.6 17.1 %collective-permute-start.1 = (bf16[16,2560]{1,0:T(8,128)(2,1)}, bf16[16,2560]{1,0:T(8,128)(2,1)S(1)}, u32[]{:S(2)}, u32[]{:S(2)}) collective-permute-start(bf16[16,2560]{1,0:T(8,128)(2,1)} %own.4), channel_id=1, source_target_pairs={{0,64},{2,66},{4,68},{6,70},{8,72},{10,74},{12,76},{14,78},{16,80}... | collective-permute-start | bytes 245768 | tf_op jit(solution)/shard_map/ppermute | solution.py:520
  2.0 15.8 %collective-permute-start.2 = (bf16[16,2560]{1,0:T(8,128)(2,1)}, bf16[16,2560]{1,0:T(8,128)(2,1)S(1)}, u32[]{:S(2)}, u32[]{:S(2)}) collective-permute-start(bf16[16,2560]{1,0:T(8,128)(2,1)} %own.4), channel_id=1, source_target_pairs={{0,65},{1,64},{2,67},{3,66},{4,69},{5,68},{6,71},{7,70},{8,73},{9,... | collective-permute-start | bytes 245768 | tf_op jit(solution)/shard_map/ppermute | solution.py:521
  3.9 11.9 %copy-start.29 = (s32[64]{0:T(128)S(1)}, s32[64]{0:T(128)}, u32[]{:S(2)}) copy-start(s32[64]{0:T(128)} %param.11) | copy-start | bytes 772
  3.9 13.7 %copy-start.28 = (f32[2560]{0:T(1024)S(1)}, f32[2560]{0:T(1024)}, u32[]{:S(2)}) copy-start(f32[2560]{0:T(1024)} %param.12) | copy-start | bytes 30724
  4.0 13.8 %copy-start.9 = (bf16[16,2560]{1,0:T(8,128)(2,1)S(1)}, bf16[16,2560]{1,0:T(8,128)(2,1)}, u32[]{:S(2)}) copy-start(bf16[16,2560]{1,0:T(8,128)(2,1)} %own.4) | copy-start | bytes 245764
  4.0 13.8 %copy-start.13 = (f32[128]{0:T(128)S(1)}, f32[128]{0:T(128)}, u32[]{:S(2)}) copy-start(f32[128]{0:T(128)} %param.17) | copy-start | bytes 1540
  4.0 13.8 %copy-start.15 = (f32[128]{0:T(128)S(1)}, f32[128]{0:T(128)}, u32[]{:S(2)}) copy-start(f32[128]{0:T(128)} %param.16) | copy-start | bytes 1540
  4.0 13.7 %collective-permute-start = (bf16[32,2560]{1,0:T(8,128)(2,1)S(1)}, bf16[32,2560]{1,0:T(8,128)(2,1)S(1)}, u32[]{:S(2)}, u32[]{:S(2)}) collective-permute-start(bf16[32,2560]{1,0:T(8,128)(2,1)S(1)} %concatenate.22), channel_id=1, source_target_pairs={{0,1},{1,0},{2,3},{3,2},{4,5},{5,4},{6,7},{7,6},{8,9},{9,8},{10,11... | collective-permute-start | bytes 491528 | tf_op jit(solution)/shard_map/ppermute | solution.py:519
  10.3 31.7 %collective-permute-start.5 = (bf16[256,2560]{1,0:T(8,128)(2,1)}, bf16[256,2560]{1,0:T(8,128)(2,1)}, u32[]{:S(2)}, u32[]{:S(2)}) collective-permute-start(bf16[256,2560]{1,0:T(8,128)(2,1)} %get-tuple-element.124), channel_id=1, source_target_pairs={{0,1},{1,0},{2,3},{3,2},{4,5},{5,4},{6,7},{7,6},{8,9},{9,8},{10,11... | collective-permute-start | bytes 3932168 | tf_op jit(solution)/shard_map/ppermute | solution.py:523
  11.0 58.9 %collective-permute-start.7 = (bf16[256,2560]{1,0:T(8,128)(2,1)}, bf16[256,2560]{1,0:T(8,128)(2,1)}, u32[]{:S(2)}, u32[]{:S(2)}) collective-permute-start(bf16[256,2560]{1,0:T(8,128)(2,1)} %get-tuple-element.123), channel_id=1, source_target_pairs={{0,1},{1,0}} | collective-permute-start | bytes 3932168 | tf_op jit(solution)/shard_map/ppermute | solution.py:524
  17.6 52.3 %copy-start.14 = (s32[2]{0:T(128)}, s32[2]{0:T(128)S(1)}, u32[]{:S(2)}) copy-start(s32[2]{0:T(128)S(1)} %pad_add_fusion.1.place) | copy-start | bytes 28
  17.6 52.3 %copy-start.11 = (f32[1,2560]{1,0:T(1,128)}, f32[1,2560]{1,0:T(1,128)S(1)}, u32[]{:S(2)}) copy-start(f32[1,2560]{1,0:T(1,128)S(1)} %reshape.137.gain_own) | copy-start | bytes 30724
  17.7 52.1 %copy-start.12 = (f32[1,2560]{1,0:T(1,128)}, f32[1,2560]{1,0:T(1,128)S(1)}, u32[]{:S(2)}) copy-start(f32[1,2560]{1,0:T(1,128)S(1)} %fusion.2.gain_other) | copy-start | bytes 30724
  17.8 24.2 %copy-start.1 = (bf16[5120,256]{1,0:T(8,128)(2,1)S(1)}, bf16[5120,256]{1,0:T(8,128)(2,1)}, u32[]{:S(2)}) copy-start(bf16[5120,256]{1,0:T(8,128)(2,1)} %rest_4_.5) | copy-start | bytes 7864324
  17.8 24.2 %copy-start.2 = (bf16[5120,256]{1,0:T(8,128)(2,1)S(1)}, bf16[5120,256]{1,0:T(8,128)(2,1)}, u32[]{:S(2)}) copy-start(bf16[5120,256]{1,0:T(8,128)(2,1)} %rest_5_.1) | copy-start | bytes 7864324
  26.9 5.5 %collective-permute-start.3 = (bf16[32,1792]{1,0:T(8,128)(2,1)S(1)}, bf16[32,1792]{1,0:T(8,128)(2,1)S(1)}, u32[]{:S(2)}, u32[]{:S(2)}) collective-permute-start(bf16[32,1792]{1,0:T(8,128)(2,1)S(1)} %shard_map.104.refs_0_.q), channel_id=1, source_target_pairs={{0,16},{2,18},{4,20},{6,22},{8,24},{10,26},{12,28},{14,30},{16,0},... | collective-permute-start | bytes 344072 | tf_op jit(solution)/shard_map/ppermute | solution.py:546
  28.7 13.3 %copy-start = (bf16[512,2560]{1,0:T(8,128)(2,1)S(1)}, bf16[512,2560]{1,0:T(8,128)(2,1)}, u32[]{:S(2)}) copy-start(bf16[512,2560]{1,0:T(8,128)(2,1)} %own.7) | copy-start | bytes 7864324
  28.9 48.3 %copy-start.3 = (f32[512,128]{1,0:T(8,128)}, f32[512,128]{1,0:T(8,128)S(1)}, u32[]{:S(2)}) copy-start(f32[512,128]{1,0:T(8,128)S(1)} %pad_maximum_fusion.rest_1_.cos.rest_2_) | copy-start | bytes 786436
  29.0 48.2 %copy-start.5 = (f32[512,128]{1,0:T(8,128)}, f32[512,128]{1,0:T(8,128)S(1)}, u32[]{:S(2)}) copy-start(f32[512,128]{1,0:T(8,128)S(1)} %pad_maximum_fusion.1.rest_2_.sin.rest_3_) | copy-start | bytes 786436
  32.4 7.6 %collective-permute-start.4 = (bf16[64,1792]{1,0:T(8,128)(2,1)S(1)}, bf16[64,1792]{1,0:T(8,128)(2,1)S(1)}, u32[]{:S(2)}, u32[]{:S(2)}) collective-permute-start(bf16[64,1792]{1,0:T(8,128)(2,1)S(1)} %shard_map.105.refs_0_), channel_id=1, source_target_pairs={{0,32},{2,34},{4,36},{6,38},{8,40},{10,42},{12,44},{14,46},{16,48}... | collective-permute-start | bytes 688136 | tf_op jit(solution)/shard_map/ppermute | solution.py:546
  40.0 8.6 %collective-permute-start.6 = (bf16[128,1792]{1,0:T(8,128)(2,1)S(1)}, bf16[128,1792]{1,0:T(8,128)(2,1)S(1)}, u32[]{:S(2)}, u32[]{:S(2)}) collective-permute-start(bf16[128,1792]{1,0:T(8,128)(2,1)S(1)} %shard_map.106.refs_0_), channel_id=1, source_target_pairs={{0,4},{2,6},{4,0},{6,2},{8,12},{10,14},{12,8},{14,10},{16,20},{18,... | collective-permute-start | bytes 1376264 | tf_op jit(solution)/shard_map/ppermute | solution.py:546
  40.1 45.4 %collective-permute-start.9 = (bf16[256,2560]{1,0:T(8,128)(2,1)}, bf16[256,2560]{1,0:T(8,128)(2,1)S(1)}, u32[]{:S(2)}, u32[]{:S(2)}) collective-permute-start(bf16[256,2560]{1,0:T(8,128)(2,1)} %get-tuple-element.123), channel_id=1, source_target_pairs={{2,3},{3,2},{4,5},{5,4},{6,7},{7,6},{8,9},{9,8},{10,11},{11,10},{1... | collective-permute-start | bytes 3932168 | tf_op jit(solution)/shard_map/ppermute | solution.py:525
  48.7 28.5 %copy-start.16 = (f32[128]{0:T(128)S(1)}, f32[128]{0:T(128)}, u32[]{:S(2)}) copy-start(f32[128]{0:T(128)} %param.16) | copy-start | bytes 1540
  48.7 37.8 %collective-permute-start.10 = (bf16[256,1792]{1,0:T(8,128)(2,1)S(1)}, bf16[256,1792]{1,0:T(8,128)(2,1)S(1)}, u32[]{:S(2)}, u32[]{:S(2)}) collective-permute-start(bf16[256,1792]{1,0:T(8,128)(2,1)S(1)} %shard_map.108.refs_0_), channel_id=1, source_target_pairs={{0,8},{2,10},{4,12},{6,14},{8,0},{10,2},{12,4},{14,6},{16,24},{18,... | collective-permute-start | bytes 2752520 | tf_op jit(solution)/shard_map/ppermute | solution.py:546
  75.9 9.7 %collective-permute-start.8 = (bf16[512,512]{1,0:T(8,128)(2,1)S(1)}, bf16[512,512]{1,0:T(8,128)(2,1)S(1)}, u32[]{:S(2)}, u32[]{:S(2)}) collective-permute-start(bf16[512,512]{1,0:T(8,128)(2,1)S(1)} %shard_map.110), channel_id=1, source_target_pairs={{0,8},{1,9}} | collective-permute-start | bytes 1572872 | tf_op jit(solution)/shard_map/ppermute | solution.py:564
  87.0 10.6 %collective-permute-start.12 = (bf16[512,1792]{1,0:T(8,128)(2,1)S(1)}, bf16[512,1792]{1,0:T(8,128)(2,1)}, u32[]{:S(2)}, u32[]{:S(2)}) collective-permute-start(bf16[512,1792]{1,0:T(8,128)(2,1)S(1)} %shard_map.112.q.kv), channel_id=1, source_target_pairs={{0,2},{2,0},{4,6},{6,4},{8,10},{10,8},{12,14},{14,12},{16,18},{18,... | collective-permute-start | bytes 5505032 | tf_op jit(solution)/shard_map/ppermute | solution.py:576
  87.1 10.4 %copy-start.23 = (bf16[512,512]{1,0:T(8,128)(2,1)}, bf16[512,512]{1,0:T(8,128)(2,1)S(1)}, u32[]{:S(2)}) copy-start(bf16[512,512]{1,0:T(8,128)(2,1)S(1)} %broadcast_select_fusion.5) | copy-start | bytes 1572868
  87.1 10.4 %collective-permute-start.11 = (bf16[512,512]{1,0:T(8,128)(2,1)S(1)}, bf16[512,512]{1,0:T(8,128)(2,1)S(1)}, u32[]{:S(2)}, u32[]{:S(2)}) collective-permute-start(bf16[512,512]{1,0:T(8,128)(2,1)S(1)} %broadcast_select_fusion.5), channel_id=1, source_target_pairs={{0,4},{8,12},{1,5},{9,13}} | collective-permute-start | bytes 1572872 | tf_op jit(solution)/shard_map/ppermute | solution.py:564
  97.6 7.5 %copy-start.26 = (bf16[512,512]{1,0:T(8,128)(2,1)}, bf16[512,512]{1,0:T(8,128)(2,1)S(1)}, u32[]{:S(2)}) copy-start(bf16[512,512]{1,0:T(8,128)(2,1)S(1)} %collective-permute-done.11) | copy-start | bytes 1572868
  98.8 6.5 %copy-start.24 = (bf16[512,512]{1,0:T(8,128)(2,1)S(1)}, bf16[512,512]{1,0:T(8,128)(2,1)}, u32[]{:S(2)}) copy-start(bf16[512,512]{1,0:T(8,128)(2,1)} %copy-done.23) | copy-start | bytes 1572868
  105.1 5.8 %collective-permute-start.13 = (bf16[512,1408]{1,0:T(8,128)(2,1)}, bf16[512,1408]{1,0:T(8,128)(2,1)}, u32[]{:S(2)}, u32[]{:S(2)}) collective-permute-start(bf16[512,1408]{1,0:T(8,128)(2,1)} %shard_map.116), channel_id=1, source_target_pairs={{0,2},{2,0},{4,6},{6,4},{8,10},{10,8},{12,14},{14,12},{16,18},{18,... | collective-permute-start | bytes 4325384 | tf_op jit(solution)/shard_map/ppermute | solution.py:585
  105.4 14.5 %collective-permute-start.14 = (bf16[512,512]{1,0:T(8,128)(2,1)S(1)}, bf16[512,512]{1,0:T(8,128)(2,1)S(1)}, u32[]{:S(2)}, u32[]{:S(2)}) collective-permute-start(bf16[512,512]{1,0:T(8,128)(2,1)S(1)} %broadcast_select_fusion.4), channel_id=1, source_target_pairs={{0,32},{4,36},{8,40},{12,44},{1,33},{5,37},{9,41},{13,45}} | collective-permute-start | bytes 1572872 | tf_op jit(solution)/shard_map/ppermute | solution.py:564
  110.9 10.4 %copy-start.18 = (bf16[256,5120]{1,0:T(8,128)(2,1)S(1)}, bf16[256,5120]{1,0:T(8,128)(2,1)}, u32[]{:S(2)}) copy-start(bf16[256,5120]{1,0:T(8,128)(2,1)} %get-tuple-element.94.normed) | copy-start | bytes 7864324
  115.1 6.2 %copy-start.4 = (f32[512,128]{1,0:T(8,128)S(1)}, f32[512,128]{1,0:T(8,128)}, u32[]{:S(2)}) copy-start(f32[512,128]{1,0:T(8,128)} %copy-done.3) | copy-start | bytes 786436
  115.1 6.2 %copy-start.6 = (f32[512,128]{1,0:T(8,128)S(1)}, f32[512,128]{1,0:T(8,128)}, u32[]{:S(2)}) copy-start(f32[512,128]{1,0:T(8,128)} %copy-done.5) | copy-start | bytes 786436
  115.1 6.2 %copy-start.17 = (f32[128]{0:T(128)S(1)}, f32[128]{0:T(128)}, u32[]{:S(2)}) copy-start(f32[128]{0:T(128)} %param.16) | copy-start | bytes 1540
  115.1 18.3 %collective-permute-start.15 = (bf16[128,1408]{1,0:T(8,128)(2,1)S(1)}, bf16[128,1408]{1,0:T(8,128)(2,1)S(1)}, u32[]{:S(2)}, u32[]{:S(2)}) collective-permute-start(bf16[128,1408]{1,0:T(8,128)(2,1)S(1)} %get-tuple-element.88), channel_id=1, source_target_pairs={{0,4},{2,6},{4,0},{6,2},{8,12},{10,14},{12,8},{14,10},{16,20},{18,... | collective-permute-start | bytes 1081352 | tf_op jit(solution)/shard_map/ppermute | solution.py:471
  116.2 18.2 %collective-permute-start.16 = (bf16[128,1408]{1,0:T(8,128)(2,1)S(1)}, bf16[128,1408]{1,0:T(8,128)(2,1)S(1)}, u32[]{:S(2)}, u32[]{:S(2)}) collective-permute-start(bf16[128,1408]{1,0:T(8,128)(2,1)S(1)} %get-tuple-element.89), channel_id=1, source_target_pairs={{0,8},{2,10},{4,12},{6,14},{8,0},{10,2},{12,4},{14,6},{16,24},{18,... | collective-permute-start | bytes 1081352 | tf_op jit(solution)/shard_map/ppermute | solution.py:471
  119.1 17.9 %collective-permute-start.17 = (bf16[128,1408]{1,0:T(8,128)(2,1)S(1)}, bf16[128,1408]{1,0:T(8,128)(2,1)S(1)}, u32[]{:S(2)}, u32[]{:S(2)}) collective-permute-start(bf16[128,1408]{1,0:T(8,128)(2,1)S(1)} %get-tuple-element.90), channel_id=1, source_target_pairs={{0,12},{2,14},{4,8},{6,10},{8,4},{10,6},{12,0},{14,2},{16,28},{18,... | collective-permute-start | bytes 1081352 | tf_op jit(solution)/shard_map/ppermute | solution.py:471
  120.0 9.7 %collective-permute-start.18 = (bf16[512,512]{1,0:T(8,128)(2,1)S(1)}, bf16[512,512]{1,0:T(8,128)(2,1)S(1)}, u32[]{:S(2)}, u32[]{:S(2)}) collective-permute-start(bf16[512,512]{1,0:T(8,128)(2,1)S(1)} %broadcast_select_fusion.2), channel_id=1, source_target_pairs={{0,16},{4,20},{8,24},{12,28},{32,48},{36,52},{40,56},{44,60},{1,17... | collective-permute-start | bytes 1572872 | tf_op jit(solution)/shard_map/ppermute | solution.py:564
  129.8 8.0 %collective-permute-start.19 = (bf16[512,512]{1,0:T(8,128)(2,1)S(1)}, bf16[512,512]{1,0:T(8,128)(2,1)S(1)}, u32[]{:S(2)}, u32[]{:S(2)}) collective-permute-start(bf16[512,512]{1,0:T(8,128)(2,1)S(1)} %broadcast_select_fusion.3), channel_id=1, source_target_pairs={{0,64},{4,68},{8,72},{12,76},{16,80},{20,84},{24,88},{28,92},{32,9... | collective-permute-start | bytes 1572872 | tf_op jit(solution)/shard_map/ppermute | solution.py:564
  139.0 6.3 %copy-start.8 = (bf16[256,1280]{1,0:T(8,128)(2,1)S(1)}, bf16[256,1280]{1,0:T(8,128)(2,1)}, u32[]{:S(2)}) copy-start(bf16[256,1280]{1,0:T(8,128)(2,1)} %copy-done.7) | copy-start | bytes 1966084
  139.0 6.2 %collective-permute-start.23 = (bf16[512,512]{1,0:T(8,128)(2,1)S(1)}, bf16[512,512]{1,0:T(8,128)(2,1)S(1)}, u32[]{:S(2)}, u32[]{:S(2)}) collective-permute-start(bf16[512,512]{1,0:T(8,128)(2,1)S(1)} %broadcast_select_fusion.1), channel_id=1, source_target_pairs={{0,2},{4,6},{8,10},{12,14},{16,18},{20,22},{24,26},{28,30},{32,34}... | collective-permute-start | bytes 1572872 | tf_op jit(solution)/shard_map/ppermute | solution.py:564
  140.5 9.8 %collective-permute-start.20 = (bf16[32,1408]{1,0:T(8,128)(2,1)S(1)}, bf16[32,1408]{1,0:T(8,128)(2,1)S(1)}, u32[]{:S(2)}, u32[]{:S(2)}) collective-permute-start(bf16[32,1408]{1,0:T(8,128)(2,1)S(1)} %get-tuple-element.101), channel_id=1, source_target_pairs={{0,16},{2,18},{4,20},{6,22},{8,24},{10,26},{12,28},{14,30},{16,0},... | collective-permute-start | bytes 270344 | tf_op jit(solution)/shard_map/ppermute | solution.py:471
  141.3 9.0 %collective-permute-start.21 = (bf16[32,1408]{1,0:T(8,128)(2,1)S(1)}, bf16[32,1408]{1,0:T(8,128)(2,1)S(1)}, u32[]{:S(2)}, u32[]{:S(2)}) collective-permute-start(bf16[32,1408]{1,0:T(8,128)(2,1)S(1)} %get-tuple-element.102), channel_id=1, source_target_pairs={{0,32},{2,34},{4,36},{6,38},{8,40},{10,42},{12,44},{14,46},{16,48}... | collective-permute-start | bytes 270344 | tf_op jit(solution)/shard_map/ppermute | solution.py:471
  141.3 9.0 %collective-permute-start.22 = (bf16[32,1408]{1,0:T(8,128)(2,1)S(1)}, bf16[32,1408]{1,0:T(8,128)(2,1)S(1)}, u32[]{:S(2)}, u32[]{:S(2)}) collective-permute-start(bf16[32,1408]{1,0:T(8,128)(2,1)S(1)} %get-tuple-element.103), channel_id=1, source_target_pairs={{0,48},{2,50},{4,52},{6,54},{8,56},{10,58},{12,60},{14,62},{16,32}... | collective-permute-start | bytes 270344 | tf_op jit(solution)/shard_map/ppermute | solution.py:471
  145.4 8.1 %copy-start.22 = (bf16[256,1280]{1,0:T(8,128)(2,1)S(1)}, bf16[256,1280]{1,0:T(8,128)(2,1)}, u32[]{:S(2)}) copy-start(bf16[256,1280]{1,0:T(8,128)(2,1)} %copy-done.21) | copy-start | bytes 1966084
  150.7 9.0 %collective-permute-start.24 = (bf16[16,1408]{1,0:T(8,128)(2,1)S(1)}, bf16[16,1408]{1,0:T(8,128)(2,1)S(1)}, u32[]{:S(2)}, u32[]{:S(2)}) collective-permute-start(bf16[16,1408]{1,0:T(8,128)(2,1)S(1)} %get-tuple-element.111), channel_id=1, source_target_pairs={{0,64},{2,66},{4,68},{6,70},{8,72},{10,74},{12,76},{14,78},{16,80}... | collective-permute-start | bytes 135176 | tf_op jit(solution)/shard_map/ppermute | solution.py:611
  (7 other events, 18.8 us)
where the time goes:
time: 161 us
  Pallas kernels  76.5 us (48%)
  starting transfers between devices  35.4 us (22%)
  waiting for transfers between devices  34.1 us (21%)
  local copies, waits for them, and re-layouts  7.23 us (4%)
  other arithmetic  5.73 us (4%)
    pallas_call x3, Pallas kernels, kv_project(): pl.pallas_call(functools.partial(kv_kernel, len(others)), grid=(rows // t...  20 us
    ppermute x1, waiting for transfers between devices, local(): ahead = lax.ppermute(ctx_hidden[split:], axes, SWAP_FIRST)  17.1 us
    pallas_call x2, Pallas kernels, project_queries(): pl.pallas_call(queries_kernel, grid=(5,), out_shape=jax.ShapeDtypeStruct(...  16.7 us
    ppermute x4, waiting for transfers between devices, double(): return lax.ppermute(array, 'seq', pairs)  11.6 us
    pallas_call x2, Pallas kernels, ctx_attention(): pl.pallas_call(functools.partial(ctx_kernel, first), grid=(1,), out_shape...  11.1 us
    pallas_call x2, Pallas kernels, fin_attention(): pl.pallas_call(functools.partial(fin_kernel, first, len(kvs)), out_shape=...  10.5 us
    ppermute x6, starting transfers between devices, send_on(): lax.ppermute(array, 'seq', to(k))  9.56 us
    pallas_call x1, Pallas kernels, fin_project(): pl.pallas_call(fin_project_kernel, out_shape=jax.ShapeDtypeStruct((rows,...  9.09 us
  transfers between devices with their start and end apart: 25, of which 8 were waited for; matrix products, arithmetic and copies ran while one was open for 6% of the time, Pallas kernels for 42%

commit v1 on v0

--- a/solution.py
+++ b/solution.py
@@ -598,11 +598,11 @@
     owner = number(my_l ^ (slot % 2), my_x ^ (slot // 2 % 4), my_z ^ (slot // 8 % 4), my_c ^ (slot // 32))
     ids = (owner[:, None] * fin_count + fin_ids[None, :]).reshape(1, -1)
     own_part = self_attention(info, ids, own_qkv, gathered, across, fin_count)
-    passed, own_part, arrived = tie(passed, own_part, arrived)
-    anchor = take(4)
+    passed, own_part = tie(passed, own_part)
     partial = merge([partial[0]] + passed, 4)
     passed = send_on(partial, to_x)
-    partial, anchor = tie(partial, anchor)
+    partial, arrived = tie(partial, arrived)
+    anchor = take(4)
     arrived = send(5)
     anchor = take(5)
     ctx_out = ctx_attention(0, split, info, q_soon, anchor, kv, None)

time: 161 us -> 160 us (level)
  transfers between devices with their start and end apart: 25 -> 25, of which waited for: 8 -> 7; matrix products, arithmetic and copies ran while one was open for 6% -> 7% of each run, Pallas kernels for 42% -> 43%
where the time goes in v1:
time: 160 us; the launch traced here: 159 us
  Pallas kernels  76.5 us (48%)
  starting transfers between devices  34.8 us (22%)
  waiting for transfers between devices  33.5 us (21%)
  local copies, waits for them, and re-layouts  7.23 us (5%)
  other arithmetic  5.71 us (4%)
    pallas_call x3, Pallas kernels, kv_project(): pl.pallas_call(functools.partial(kv_kernel, len(others)), grid=(rows // t...  20 us
    ppermute x1, waiting for transfers between devices, local(): ahead = lax.ppermute(ctx_hidden[split:], axes, SWAP_FIRST)  17.1 us
    pallas_call x2, Pallas kernels, project_queries(): pl.pallas_call(queries_kernel, grid=(5,), out_shape=jax.ShapeDtypeStruct(...  16.7 us
    ppermute x4, waiting for transfers between devices, double(): return lax.ppermute(array, 'seq', pairs)  11.6 us
    pallas_call x2, Pallas kernels, ctx_attention(): pl.pallas_call(functools.partial(ctx_kernel, first), grid=(1,), out_shape...  11.1 us
    pallas_call x2, Pallas kernels, fin_attention(): pl.pallas_call(functools.partial(fin_kernel, first, len(kvs)), out_shape=...  10.5 us
    ppermute x6, starting transfers between devices, send_on(): lax.ppermute(array, 'seq', to(k))  9.56 us
    pallas_call x1, Pallas kernels, fin_project(): pl.pallas_call(fin_project_kernel, out_shape=jax.ShapeDtypeStruct((rows,...  9.09 us
  transfers between devices with their start and end apart: 25, of which 7 were waited for; matrix products, arithmetic and copies ran while one was open for 7% of the time, Pallas kernels for 43%

profile of v1, /device:TPU:16, one launch (start us, length us, event | category | flops | bytes accessed | tf_op | source)
XLA Modules:
  0.0 159.3 jit_solution(2504171339493478270)
XLA Ops:
  0.6 1.4 collective-permute-start.1
  2.0 0.7 fusion.1
  2.8 1.2 concatenate.22
  4.0 2.9 %collective-permute-start = (bf16[32,2560]{1,0:T(8,128)(2,1)S(1)}, bf16[32,2560]{1,0:T(8,128)(2,1)S(1)}, u32[]{:S(2)}, u32[]{:S(2)}) collective-permute-start(bf16[32,2560]{1,0:T(8,128)(2,1)S(1)} %concatenate.22), channel_id=1, source_target_pairs={{0,1},{1,0},{2,3},{3,2},{4,5},{5,4},{6,7},{7,6},{8,9},{9,8},{10,11... | collective-permute-start | bytes 491528 | tf_op jit(solution)/shard_map/ppermute | solution.py:519
  6.9 3.4 %fusion.20 = (bf16[256,2560]{1,0:T(8,128)(2,1)}, bf16[256,2560]{1,0:T(8,128)(2,1)}) fusion(bf16[512,2560]{1,0:T(8,128)(2,1)} %own.7), kind=kLoop, calls=%fused_computation.67 | loop fusion | bytes 5242880 | tf_op jit(solution)/shard_map/slice | solution.py:524
  10.3 0.7 collective-permute-start.5
  11.0 4.7 %collective-permute-start.7 = (bf16[256,2560]{1,0:T(8,128)(2,1)}, bf16[256,2560]{1,0:T(8,128)(2,1)}, u32[]{:S(2)}, u32[]{:S(2)}) collective-permute-start(bf16[256,2560]{1,0:T(8,128)(2,1)} %get-tuple-element.121), channel_id=1, source_target_pairs={{0,1},{1,0}} | collective-permute-start | bytes 3932168 | tf_op jit(solution)/shard_map/ppermute | solution.py:524
  15.9 0.7 fusion.7
  16.6 0.7 fusion.18
  17.8 9.1 %shard_map.104.refs_0_.q = bf16[32,1792]{1,0:T(8,128)(2,1)S(1)} custom-call(s32[2]{0:T(128)S(1)} %pad_add_fusion.1.place, bf16[16,2560]{1,0:T(8,128)(2,1)S(1)} %copy-done.9, bf16[32,2560]{1,0:T(8,128)(2,1)S(1)} %collective-permute-done.other, bf16[16,2560]{1,0:T(8,128)(2,1)S(1)} %collective-permute-done.1.near_own, ...), custom_call_target="tpu_custom_call" | custom-call | flops 115000000 | bytes 100000 | tf_op jit(solution)/shard_map/pallas_call | solution.py:124
  27.0 0.7 add_convert_fusion
  27.7 1.0 fusion
  29.0 3.3 %collective-permute-done.3.refs_1_ = bf16[32,1792]{1,0:T(8,128)(2,1)S(1)} collective-permute-done((bf16[32,1792]{1,0:T(8,128)(2,1)S(1)}, bf16[32,1792]{1,0:T(8,128)(2,1)S(1)}, u32[]{:S(2)}, u32[]{:S(2)}) %collective-permute-start.3) | collective-permute-done | bytes 114720 | tf_op jit(solution)/shard_map/ppermute | solution.py:546
  32.5 7.5 %collective-permute-done.4.refs_1_ = bf16[64,1792]{1,0:T(8,128)(2,1)S(1)} collective-permute-done((bf16[64,1792]{1,0:T(8,128)(2,1)S(1)}, bf16[64,1792]{1,0:T(8,128)(2,1)S(1)}, u32[]{:S(2)}, u32[]{:S(2)}) %collective-permute-start.4) | collective-permute-done | bytes 229408 | tf_op jit(solution)/shard_map/ppermute | solution.py:546
  40.1 0.7 collective-permute-start.9
  40.9 1.1 collective-permute-done.5.rest_0_
  42.0 5.9 %shard_map.107 = (bf16[256,512]{1,0:T(8,128)(2,1)S(1)}, bf16[256,5120]{1,0:T(8,128)(2,1)S(1)}) custom-call(s32[2]{0:T(128)S(1)} %pad_add_fusion.1.place, f32[1,2560]{1,0:T(1,128)S(1)} %reshape.137.gain_own, f32[1,2560]{1,0:T(1,128)S(1)} %fusion.2.gain_other, f32[1,128]{1,0:T(1,128)S(1)} %bitcast.8, bf16[512,2560]{1,0:T(8,128)(2,1)S(1)} %copy-done, ...), custom_call_target="tpu_custom_call" | custom-call | flops 46000000 | bytes 40000 | tf_op jit(solution)/shard_map/pallas_call | solution.py:172
  47.9 0.7 collective-permute-done.6.refs_1_
  48.7 4.1 %collective-permute-start.10 = (bf16[256,1792]{1,0:T(8,128)(2,1)S(1)}, bf16[256,1792]{1,0:T(8,128)(2,1)S(1)}, u32[]{:S(2)}, u32[]{:S(2)}) collective-permute-start(bf16[256,1792]{1,0:T(8,128)(2,1)S(1)} %shard_map.108.refs_0_), channel_id=1, source_target_pairs={{0,8},{2,10},{4,12},{6,14},{8,0},{10,2},{12,4},{14,6},{16,24},{18,... | collective-permute-start | bytes 2752520 | tf_op jit(solution)/shard_map/ppermute | solution.py:546
  52.8 17.1 %collective-permute-done.7.rest_0_.rest_1_ = bf16[256,2560]{1,0:T(8,128)(2,1)} collective-permute-done((bf16[256,2560]{1,0:T(8,128)(2,1)}, bf16[256,2560]{1,0:T(8,128)(2,1)}, u32[]{:S(2)}, u32[]{:S(2)}) %collective-permute-start.7) | collective-permute-done | bytes 1310752 | tf_op jit(solution)/shard_map/ppermute | solution.py:524
  69.9 5.9 %shard_map.109 = (bf16[256,512]{1,0:T(8,128)(2,1)S(1)}, bf16[256,5120]{1,0:T(8,128)(2,1)}) custom-call(s32[2]{0:T(128)S(1)} %pad_add_fusion.1.place, f32[1,2560]{1,0:T(1,128)S(1)} %reshape.137.gain_own, f32[1,2560]{1,0:T(1,128)S(1)} %fusion.2.gain_other, f32[1,128]{1,0:T(1,128)S(1)} %bitcast.9, bf16[512,2560]{1,0:T(8,128)(2,1)S(1)} %copy-done, ...), custom_call_target="tpu_custom_call" | custom-call | flops 46000000 | bytes 40000 | tf_op jit(solution)/shard_map/pallas_call | solution.py:172
  75.9 1.3 collective-permute-start.8
  77.2 8.3 %shard_map.111.q = bf16[256,1280]{1,0:T(8,128)(2,1)S(1)} custom-call(f32[1,128]{1,0:T(1,128)S(1)} %bitcast.11, f32[512,128]{1,0:T(8,128)S(1)} %pad_maximum_fusion.rest_1_.cos.rest_2_, f32[512,128]{1,0:T(8,128)S(1)} %pad_maximum_fusion.1.rest_2_.sin.rest_3_, bf16[5120,1280]{1,0:T(8,128)(2,1)} %wq.5, bf16[256,5120]{1,0:T(8,128)(2,1)S(1)} %get-tuple-element.75.normed), custom_call_target="tpu_custom_call" | custom-call | flops 115000000 | bytes 100000 | tf_op jit(solution)/shard_map/pallas_call | solution.py:214
  85.6 0.9 copy-done.27
  87.1 1.5 collective-permute-start.11
  88.6 0.7 pad_add_fusion.info
  89.3 8.2 %shard_map.113 = (bf16[256,512]{1,0:T(8,128)(2,1)}, bf16[256,5120]{1,0:T(8,128)(2,1)}) custom-call(s32[2]{0:T(128)} %copy-done.14, f32[1,2560]{1,0:T(1,128)} %copy-done.11, f32[1,2560]{1,0:T(1,128)} %copy-done.12, f32[1,128]{1,0:T(1,128)} %bitcast.6, bf16[512,2560]{1,0:T(8,128)(2,1)} %own.7, bf16[256,2560]{1,0:T(8,128)(2,1)} %copy-done.25, ...), custom_call_target="tpu_custom_call" | custom-call | flops 46000000 | bytes 40000 | tf_op jit(solution)/shard_map/pallas_call | solution.py:172
  97.6 1.1 copy-done.10
  98.8 6.3 %shard_map.116 = bf16[512,1408]{1,0:T(8,128)(2,1)} custom-call(s32[4]{0:T(128)S(1)} %pad_add_fusion.info, bf16[512,1792]{1,0:T(8,128)(2,1)} %collective-permute-done.12.q.kv_across, bf16[512,512]{1,0:T(8,128)(2,1)S(1)} %shard_map.114.refs_0_.kv), custom_call_target="tpu_custom_call" | custom-call | flops 5750000128 | bytes 5000000 | tf_op jit(solution)/shard_map/pallas_call | solution.py:343
  105.4 1.3 collective-permute-start.14
  106.7 4.2 %shard_map.115.refs_0_ = bf16[512,1408]{1,0:T(8,128)(2,1)S(1)} custom-call(s32[4]{0:T(128)S(1)} %pad_add_fusion.info, bf16[512,1792]{1,0:T(8,128)(2,1)S(1)} %shard_map.112.q.kv, bf16[512,512]{1,0:T(8,128)(2,1)S(1)} %shard_map.114.refs_0_.kv), custom_call_target="tpu_custom_call" | custom-call | flops 5750000128 | bytes 5000000 | tf_op jit(solution)/shard_map/pallas_call | solution.py:343
  110.9 4.1 %shard_map.117 = (bf16[128,1408]{1,0:T(8,128)(2,1)S(1)}, bf16[128,1408]{1,0:T(8,128)(2,1)S(1)}, bf16[128,1408]{1,0:T(8,128)(2,1)S(1)}, bf16[128,1408]{1,0:T(8,128)(2,1)S(1)}) custom-call(s32[1]{0:T(128)} %constant.135.clone.1.info, bf16[512,1408]{1,0:T(8,128)(2,1)S(1)} %shard_map.115.refs_0_, bf16[512,1408]{1,0:T(8,128)(2,1)} %collective-permute-done.13.refs_1_), custom_call_target="tpu_custom_call" | custom-call | flops 2760000000 | bytes 2400000 | tf_op jit(solution)/shard_map/pallas_call | solution.py:442
  115.1 1.1 collective-permute-start.15
  116.2 2.9 %collective-permute-start.16 = (bf16[128,1408]{1,0:T(8,128)(2,1)S(1)}, bf16[128,1408]{1,0:T(8,128)(2,1)S(1)}, u32[]{:S(2)}, u32[]{:S(2)}) collective-permute-start(bf16[128,1408]{1,0:T(8,128)(2,1)S(1)} %get-tuple-element.88), channel_id=1, source_target_pairs={{0,8},{2,10},{4,12},{6,14},{8,0},{10,2},{12,4},{14,6},{16,24},{18,... | collective-permute-start | bytes 1081352 | tf_op jit(solution)/shard_map/ppermute | solution.py:471
  119.1 0.8 collective-permute-start.17
  120.0 1.3 collective-permute-start.18
  121.3 8.3 %shard_map.120.q = bf16[256,1280]{1,0:T(8,128)(2,1)S(1)} custom-call(f32[1,128]{1,0:T(1,128)S(1)} %bitcast.12, f32[512,128]{1,0:T(8,128)S(1)} %copy-done.4, f32[512,128]{1,0:T(8,128)S(1)} %copy-done.6, bf16[5120,1280]{1,0:T(8,128)(2,1)} %wq.5, bf16[256,5120]{1,0:T(8,128)(2,1)S(1)} %copy-done.18), custom_call_target="tpu_custom_call" | custom-call | flops 9200000000 | bytes 8000000 | tf_op jit(solution)/shard_map/pallas_call | solution.py:214
  129.8 1.3 collective-permute-start.19
  131.1 2.3 %shard_map.118.refs_2_ = bf16[16,1408]{1,0:T(8,128)(2,1)S(1)} custom-call(s32[4]{0:T(128)S(1)} %pad_add_fusion.info, s32[1,1024]{1,0:T(1,128)S(1)} %add.184.ids, bf16[32,1792]{1,0:T(8,128)(2,1)S(1)} %shard_map.104.refs_0_.q, bf16[512,1792]{1,0:T(8,128)(2,1)S(1)} %shard_map.112.q.kv, bf16[512,1792]{1,0:T(8,128)(2,1)} %collective-permute-done.12.q.kv_across), custom_call_target="tpu_custom_call" | custom-call | flops 5750000128 | bytes 5000000 | tf_op jit(solution)/shard_map/pallas_call | solution.py:393
  133.4 1.0 collective-permute-done.16.refs_2_
  134.4 2.7 %collective-permute-done.17.refs_3_ = bf16[128,1408]{1,0:T(8,128)(2,1)S(1)} collective-permute-done((bf16[128,1408]{1,0:T(8,128)(2,1)S(1)}, bf16[128,1408]{1,0:T(8,128)(2,1)S(1)}, u32[]{:S(2)}, u32[]{:S(2)}) %collective-permute-start.17) | collective-permute-done | bytes 360480 | tf_op jit(solution)/shard_map/ppermute | solution.py:471
  137.1 1.2 shard_map.119
  138.4 1.5 collective-permute-start.23
  140.1 4.5 %collective-permute-start.22 = (bf16[32,1408]{1,0:T(8,128)(2,1)S(1)}, bf16[32,1408]{1,0:T(8,128)(2,1)S(1)}, u32[]{:S(2)}, u32[]{:S(2)}) collective-permute-start(bf16[32,1408]{1,0:T(8,128)(2,1)S(1)} %get-tuple-element.99), channel_id=1, source_target_pairs={{0,48},{2,50},{4,52},{6,54},{8,56},{10,58},{12,60},{14,62},{16,32}... | collective-permute-start | bytes 270344 | tf_op jit(solution)/shard_map/ppermute | solution.py:471
  144.7 5.0 %shard_map.121.refs_0_ = bf16[512,1280]{1,0:T(8,128)(2,1)} custom-call(s32[4]{0:T(128)S(1)} %pad_add_fusion.info, bf16[512,512]{1,0:T(8,128)(2,1)S(1)} %broadcast_select_fusion.1.anchor, bf16[256,1280]{1,0:T(8,128)(2,1)S(1)} %copy-done.8, bf16[512,512]{1,0:T(8,128)(2,1)S(1)} %shard_map.114.refs_0_.kv), custom_call_target="tpu_custom_call" | custom-call | flops 5750000128 | bytes 5000000 | tf_op jit(solution)/shard_map/pallas_call | solution.py:285
  150.0 2.3 %collective-permute-start.24 = (bf16[16,1408]{1,0:T(8,128)(2,1)S(1)}, bf16[16,1408]{1,0:T(8,128)(2,1)S(1)}, u32[]{:S(2)}, u32[]{:S(2)}) collective-permute-start(bf16[16,1408]{1,0:T(8,128)(2,1)S(1)} %get-tuple-element.109), channel_id=1, source_target_pairs={{0,64},{2,66},{4,68},{6,70},{8,72},{10,74},{12,76},{14,78},{16,80}... | collective-permute-start | bytes 135176 | tf_op jit(solution)/shard_map/ppermute | solution.py:611
  152.2 6.2 %shard_map.123 = bf16[512,1280]{1,0:T(8,128)(2,1)} custom-call(s32[4]{0:T(128)S(1)} %pad_add_fusion.info, bf16[512,512]{1,0:T(8,128)(2,1)S(1)} %broadcast_select_fusion.1.anchor, bf16[256,1280]{1,0:T(8,128)(2,1)S(1)} %copy-done.22, bf16[512,512]{1,0:T(8,128)(2,1)S(1)} %shard_map.114.refs_0_.kv, ...), custom_call_target="tpu_custom_call", output_to_operand_aliasing={{}: (4, {})} | custom-call | flops 5750000128 | bytes 5000000 | tf_op jit(solution)/shard_map/pallas_call | solution.py:285
  158.4 0.9 shard_map.124
  (114 shorter events, 3.0 us)
Async XLA Ops:
  0.6 17.1 %collective-permute-start.1 = (bf16[16,2560]{1,0:T(8,128)(2,1)}, bf16[16,2560]{1,0:T(8,128)(2,1)S(1)}, u32[]{:S(2)}, u32[]{:S(2)}) collective-permute-start(bf16[16,2560]{1,0:T(8,128)(2,1)} %own.4), channel_id=1, source_target_pairs={{0,64},{2,66},{4,68},{6,70},{8,72},{10,74},{12,76},{14,78},{16,80}... | collective-permute-start | bytes 245768 | tf_op jit(solution)/shard_map/ppermute | solution.py:520
  2.0 15.8 %collective-permute-start.2 = (bf16[16,2560]{1,0:T(8,128)(2,1)}, bf16[16,2560]{1,0:T(8,128)(2,1)S(1)}, u32[]{:S(2)}, u32[]{:S(2)}) collective-permute-start(bf16[16,2560]{1,0:T(8,128)(2,1)} %own.4), channel_id=1, source_target_pairs={{0,65},{1,64},{2,67},{3,66},{4,69},{5,68},{6,71},{7,70},{8,73},{9,... | collective-permute-start | bytes 245768 | tf_op jit(solution)/shard_map/ppermute | solution.py:521
  3.9 11.9 %copy-start.29 = (s32[64]{0:T(128)S(1)}, s32[64]{0:T(128)}, u32[]{:S(2)}) copy-start(s32[64]{0:T(128)} %param.11) | copy-start | bytes 772
  3.9 13.7 %copy-start.28 = (f32[2560]{0:T(1024)S(1)}, f32[2560]{0:T(1024)}, u32[]{:S(2)}) copy-start(f32[2560]{0:T(1024)} %param.12) | copy-start | bytes 30724
  4.0 13.8 %copy-start.9 = (bf16[16,2560]{1,0:T(8,128)(2,1)S(1)}, bf16[16,2560]{1,0:T(8,128)(2,1)}, u32[]{:S(2)}) copy-start(bf16[16,2560]{1,0:T(8,128)(2,1)} %own.4) | copy-start | bytes 245764
  4.0 13.8 %copy-start.13 = (f32[128]{0:T(128)S(1)}, f32[128]{0:T(128)}, u32[]{:S(2)}) copy-start(f32[128]{0:T(128)} %param.17) | copy-start | bytes 1540
  4.0 13.8 %copy-start.15 = (f32[128]{0:T(128)S(1)}, f32[128]{0:T(128)}, u32[]{:S(2)}) copy-start(f32[128]{0:T(128)} %param.16) | copy-start | bytes 1540
  4.0 13.7 %collective-permute-start = (bf16[32,2560]{1,0:T(8,128)(2,1)S(1)}, bf16[32,2560]{1,0:T(8,128)(2,1)S(1)}, u32[]{:S(2)}, u32[]{:S(2)}) collective-permute-start(bf16[32,2560]{1,0:T(8,128)(2,1)S(1)} %concatenate.22), channel_id=1, source_target_pairs={{0,1},{1,0},{2,3},{3,2},{4,5},{5,4},{6,7},{7,6},{8,9},{9,8},{10,11... | collective-permute-start | bytes 491528 | tf_op jit(solution)/shard_map/ppermute | solution.py:519
  10.3 31.7 %collective-permute-start.5 = (bf16[256,2560]{1,0:T(8,128)(2,1)}, bf16[256,2560]{1,0:T(8,128)(2,1)}, u32[]{:S(2)}, u32[]{:S(2)}) collective-permute-start(bf16[256,2560]{1,0:T(8,128)(2,1)} %get-tuple-element.122), channel_id=1, source_target_pairs={{0,1},{1,0},{2,3},{3,2},{4,5},{5,4},{6,7},{7,6},{8,9},{9,8},{10,11... | collective-permute-start | bytes 3932168 | tf_op jit(solution)/shard_map/ppermute | solution.py:523
  11.0 58.9 %collective-permute-start.7 = (bf16[256,2560]{1,0:T(8,128)(2,1)}, bf16[256,2560]{1,0:T(8,128)(2,1)}, u32[]{:S(2)}, u32[]{:S(2)}) collective-permute-start(bf16[256,2560]{1,0:T(8,128)(2,1)} %get-tuple-element.121), channel_id=1, source_target_pairs={{0,1},{1,0}} | collective-permute-start | bytes 3932168 | tf_op jit(solution)/shard_map/ppermute | solution.py:524
  17.6 52.3 %copy-start.14 = (s32[2]{0:T(128)}, s32[2]{0:T(128)S(1)}, u32[]{:S(2)}) copy-start(s32[2]{0:T(128)S(1)} %pad_add_fusion.1.place) | copy-start | bytes 28
  17.6 52.3 %copy-start.11 = (f32[1,2560]{1,0:T(1,128)}, f32[1,2560]{1,0:T(1,128)S(1)}, u32[]{:S(2)}) copy-start(f32[1,2560]{1,0:T(1,128)S(1)} %reshape.137.gain_own) | copy-start | bytes 30724
  17.7 52.1 %copy-start.12 = (f32[1,2560]{1,0:T(1,128)}, f32[1,2560]{1,0:T(1,128)S(1)}, u32[]{:S(2)}) copy-start(f32[1,2560]{1,0:T(1,128)S(1)} %fusion.2.gain_other) | copy-start | bytes 30724
  17.8 24.2 %copy-start.1 = (bf16[5120,256]{1,0:T(8,128)(2,1)S(1)}, bf16[5120,256]{1,0:T(8,128)(2,1)}, u32[]{:S(2)}) copy-start(bf16[5120,256]{1,0:T(8,128)(2,1)} %rest_4_.5) | copy-start | bytes 7864324
  17.8 24.2 %copy-start.2 = (bf16[5120,256]{1,0:T(8,128)(2,1)S(1)}, bf16[5120,256]{1,0:T(8,128)(2,1)}, u32[]{:S(2)}) copy-start(bf16[5120,256]{1,0:T(8,128)(2,1)} %rest_5_.1) | copy-start | bytes 7864324
  26.9 5.5 %collective-permute-start.3 = (bf16[32,1792]{1,0:T(8,128)(2,1)S(1)}, bf16[32,1792]{1,0:T(8,128)(2,1)S(1)}, u32[]{:S(2)}, u32[]{:S(2)}) collective-permute-start(bf16[32,1792]{1,0:T(8,128)(2,1)S(1)} %shard_map.104.refs_0_.q), channel_id=1, source_target_pairs={{0,16},{2,18},{4,20},{6,22},{8,24},{10,26},{12,28},{14,30},{16,0},... | collective-permute-start | bytes 344072 | tf_op jit(solution)/shard_map/ppermute | solution.py:546
  28.7 13.3 %copy-start = (bf16[512,2560]{1,0:T(8,128)(2,1)S(1)}, bf16[512,2560]{1,0:T(8,128)(2,1)}, u32[]{:S(2)}) copy-start(bf16[512,2560]{1,0:T(8,128)(2,1)} %own.7) | copy-start | bytes 7864324
  28.9 48.3 %copy-start.3 = (f32[512,128]{1,0:T(8,128)}, f32[512,128]{1,0:T(8,128)S(1)}, u32[]{:S(2)}) copy-start(f32[512,128]{1,0:T(8,128)S(1)} %pad_maximum_fusion.rest_1_.cos.rest_2_) | copy-start | bytes 786436
  29.0 48.2 %copy-start.5 = (f32[512,128]{1,0:T(8,128)}, f32[512,128]{1,0:T(8,128)S(1)}, u32[]{:S(2)}) copy-start(f32[512,128]{1,0:T(8,128)S(1)} %pad_maximum_fusion.1.rest_2_.sin.rest_3_) | copy-start | bytes 786436
  32.4 7.6 %collective-permute-start.4 = (bf16[64,1792]{1,0:T(8,128)(2,1)S(1)}, bf16[64,1792]{1,0:T(8,128)(2,1)S(1)}, u32[]{:S(2)}, u32[]{:S(2)}) collective-permute-start(bf16[64,1792]{1,0:T(8,128)(2,1)S(1)} %shard_map.105.refs_0_), channel_id=1, source_target_pairs={{0,32},{2,34},{4,36},{6,38},{8,40},{10,42},{12,44},{14,46},{16,48}... | collective-permute-start | bytes 688136 | tf_op jit(solution)/shard_map/ppermute | solution.py:546
  40.0 8.6 %collective-permute-start.6 = (bf16[128,1792]{1,0:T(8,128)(2,1)S(1)}, bf16[128,1792]{1,0:T(8,128)(2,1)S(1)}, u32[]{:S(2)}, u32[]{:S(2)}) collective-permute-start(bf16[128,1792]{1,0:T(8,128)(2,1)S(1)} %shard_map.106.refs_0_), channel_id=1, source_target_pairs={{0,4},{2,6},{4,0},{6,2},{8,12},{10,14},{12,8},{14,10},{16,20},{18,... | collective-permute-start | bytes 1376264 | tf_op jit(solution)/shard_map/ppermute | solution.py:546
  40.1 45.4 %collective-permute-start.9 = (bf16[256,2560]{1,0:T(8,128)(2,1)}, bf16[256,2560]{1,0:T(8,128)(2,1)S(1)}, u32[]{:S(2)}, u32[]{:S(2)}) collective-permute-start(bf16[256,2560]{1,0:T(8,128)(2,1)} %get-tuple-element.121), channel_id=1, source_target_pairs={{2,3},{3,2},{4,5},{5,4},{6,7},{7,6},{8,9},{9,8},{10,11},{11,10},{1... | collective-permute-start | bytes 3932168 | tf_op jit(solution)/shard_map/ppermute | solution.py:525
  48.7 28.5 %copy-start.16 = (f32[128]{0:T(128)S(1)}, f32[128]{0:T(128)}, u32[]{:S(2)}) copy-start(f32[128]{0:T(128)} %param.16) | copy-start | bytes 1540
  48.7 37.8 %collective-permute-start.10 = (bf16[256,1792]{1,0:T(8,128)(2,1)S(1)}, bf16[256,1792]{1,0:T(8,128)(2,1)S(1)}, u32[]{:S(2)}, u32[]{:S(2)}) collective-permute-start(bf16[256,1792]{1,0:T(8,128)(2,1)S(1)} %shard_map.108.refs_0_), channel_id=1, source_target_pairs={{0,8},{2,10},{4,12},{6,14},{8,0},{10,2},{12,4},{14,6},{16,24},{18,... | collective-permute-start | bytes 2752520 | tf_op jit(solution)/shard_map/ppermute | solution.py:546
  75.9 9.7 %collective-permute-start.8 = (bf16[512,512]{1,0:T(8,128)(2,1)S(1)}, bf16[512,512]{1,0:T(8,128)(2,1)S(1)}, u32[]{:S(2)}, u32[]{:S(2)}) collective-permute-start(bf16[512,512]{1,0:T(8,128)(2,1)S(1)} %shard_map.110), channel_id=1, source_target_pairs={{0,8},{1,9}} | collective-permute-start | bytes 1572872 | tf_op jit(solution)/shard_map/ppermute | solution.py:564
  87.0 10.6 %collective-permute-start.12 = (bf16[512,1792]{1,0:T(8,128)(2,1)S(1)}, bf16[512,1792]{1,0:T(8,128)(2,1)}, u32[]{:S(2)}, u32[]{:S(2)}) collective-permute-start(bf16[512,1792]{1,0:T(8,128)(2,1)S(1)} %shard_map.112.q.kv), channel_id=1, source_target_pairs={{0,2},{2,0},{4,6},{6,4},{8,10},{10,8},{12,14},{14,12},{16,18},{18,... | collective-permute-start | bytes 5505032 | tf_op jit(solution)/shard_map/ppermute | solution.py:576
  87.1 10.4 %copy-start.23 = (bf16[512,512]{1,0:T(8,128)(2,1)}, bf16[512,512]{1,0:T(8,128)(2,1)S(1)}, u32[]{:S(2)}) copy-start(bf16[512,512]{1,0:T(8,128)(2,1)S(1)} %broadcast_select_fusion.5) | copy-start | bytes 1572868
  87.1 10.4 %collective-permute-start.11 = (bf16[512,512]{1,0:T(8,128)(2,1)S(1)}, bf16[512,512]{1,0:T(8,128)(2,1)S(1)}, u32[]{:S(2)}, u32[]{:S(2)}) collective-permute-start(bf16[512,512]{1,0:T(8,128)(2,1)S(1)} %broadcast_select_fusion.5), channel_id=1, source_target_pairs={{0,4},{8,12},{1,5},{9,13}} | collective-permute-start | bytes 1572872 | tf_op jit(solution)/shard_map/ppermute | solution.py:564
  97.6 7.5 %copy-start.26 = (bf16[512,512]{1,0:T(8,128)(2,1)}, bf16[512,512]{1,0:T(8,128)(2,1)S(1)}, u32[]{:S(2)}) copy-start(bf16[512,512]{1,0:T(8,128)(2,1)S(1)} %collective-permute-done.11) | copy-start | bytes 1572868
  98.8 6.5 %copy-start.24 = (bf16[512,512]{1,0:T(8,128)(2,1)S(1)}, bf16[512,512]{1,0:T(8,128)(2,1)}, u32[]{:S(2)}) copy-start(bf16[512,512]{1,0:T(8,128)(2,1)} %copy-done.23) | copy-start | bytes 1572868
  105.1 5.8 %collective-permute-start.13 = (bf16[512,1408]{1,0:T(8,128)(2,1)}, bf16[512,1408]{1,0:T(8,128)(2,1)}, u32[]{:S(2)}, u32[]{:S(2)}) collective-permute-start(bf16[512,1408]{1,0:T(8,128)(2,1)} %shard_map.116), channel_id=1, source_target_pairs={{0,2},{2,0},{4,6},{6,4},{8,10},{10,8},{12,14},{14,12},{16,18},{18,... | collective-permute-start | bytes 4325384 | tf_op jit(solution)/shard_map/ppermute | solution.py:585
  105.4 14.5 %collective-permute-start.14 = (bf16[512,512]{1,0:T(8,128)(2,1)S(1)}, bf16[512,512]{1,0:T(8,128)(2,1)S(1)}, u32[]{:S(2)}, u32[]{:S(2)}) collective-permute-start(bf16[512,512]{1,0:T(8,128)(2,1)S(1)} %broadcast_select_fusion.4), channel_id=1, source_target_pairs={{0,32},{4,36},{8,40},{12,44},{1,33},{5,37},{9,41},{13,45}} | collective-permute-start | bytes 1572872 | tf_op jit(solution)/shard_map/ppermute | solution.py:564
  110.9 10.4 %copy-start.18 = (bf16[256,5120]{1,0:T(8,128)(2,1)S(1)}, bf16[256,5120]{1,0:T(8,128)(2,1)}, u32[]{:S(2)}) copy-start(bf16[256,5120]{1,0:T(8,128)(2,1)} %get-tuple-element.100.normed) | copy-start | bytes 7864324
  115.1 6.2 %copy-start.4 = (f32[512,128]{1,0:T(8,128)S(1)}, f32[512,128]{1,0:T(8,128)}, u32[]{:S(2)}) copy-start(f32[512,128]{1,0:T(8,128)} %copy-done.3) | copy-start | bytes 786436
  115.1 6.2 %copy-start.6 = (f32[512,128]{1,0:T(8,128)S(1)}, f32[512,128]{1,0:T(8,128)}, u32[]{:S(2)}) copy-start(f32[512,128]{1,0:T(8,128)} %copy-done.5) | copy-start | bytes 786436
  115.1 6.2 %copy-start.17 = (f32[128]{0:T(128)S(1)}, f32[128]{0:T(128)}, u32[]{:S(2)}) copy-start(f32[128]{0:T(128)} %param.16) | copy-start | bytes 1540
  115.1 18.3 %collective-permute-start.15 = (bf16[128,1408]{1,0:T(8,128)(2,1)S(1)}, bf16[128,1408]{1,0:T(8,128)(2,1)S(1)}, u32[]{:S(2)}, u32[]{:S(2)}) collective-permute-start(bf16[128,1408]{1,0:T(8,128)(2,1)S(1)} %get-tuple-element.87), channel_id=1, source_target_pairs={{0,4},{2,6},{4,0},{6,2},{8,12},{10,14},{12,8},{14,10},{16,20},{18,... | collective-permute-start | bytes 1081352 | tf_op jit(solution)/shard_map/ppermute | solution.py:471
  116.2 18.2 %collective-permute-start.16 = (bf16[128,1408]{1,0:T(8,128)(2,1)S(1)}, bf16[128,1408]{1,0:T(8,128)(2,1)S(1)}, u32[]{:S(2)}, u32[]{:S(2)}) collective-permute-start(bf16[128,1408]{1,0:T(8,128)(2,1)S(1)} %get-tuple-element.88), channel_id=1, source_target_pairs={{0,8},{2,10},{4,12},{6,14},{8,0},{10,2},{12,4},{14,6},{16,24},{18,... | collective-permute-start | bytes 1081352 | tf_op jit(solution)/shard_map/ppermute | solution.py:471
  119.1 17.9 %collective-permute-start.17 = (bf16[128,1408]{1,0:T(8,128)(2,1)S(1)}, bf16[128,1408]{1,0:T(8,128)(2,1)S(1)}, u32[]{:S(2)}, u32[]{:S(2)}) collective-permute-start(bf16[128,1408]{1,0:T(8,128)(2,1)S(1)} %get-tuple-element.89), channel_id=1, source_target_pairs={{0,12},{2,14},{4,8},{6,10},{8,4},{10,6},{12,0},{14,2},{16,28},{18,... | collective-permute-start | bytes 1081352 | tf_op jit(solution)/shard_map/ppermute | solution.py:471
  120.0 9.7 %collective-permute-start.18 = (bf16[512,512]{1,0:T(8,128)(2,1)S(1)}, bf16[512,512]{1,0:T(8,128)(2,1)S(1)}, u32[]{:S(2)}, u32[]{:S(2)}) collective-permute-start(bf16[512,512]{1,0:T(8,128)(2,1)S(1)} %broadcast_select_fusion.2), channel_id=1, source_target_pairs={{0,16},{4,20},{8,24},{12,28},{32,48},{36,52},{40,56},{44,60},{1,17... | collective-permute-start | bytes 1572872 | tf_op jit(solution)/shard_map/ppermute | solution.py:564
  129.8 8.5 %collective-permute-start.19 = (bf16[512,512]{1,0:T(8,128)(2,1)S(1)}, bf16[512,512]{1,0:T(8,128)(2,1)S(1)}, u32[]{:S(2)}, u32[]{:S(2)}) collective-permute-start(bf16[512,512]{1,0:T(8,128)(2,1)S(1)} %broadcast_select_fusion.3), channel_id=1, source_target_pairs={{0,64},{4,68},{8,72},{12,76},{16,80},{20,84},{24,88},{28,92},{32,9... | collective-permute-start | bytes 1572872 | tf_op jit(solution)/shard_map/ppermute | solution.py:564
  138.3 6.4 %copy-start.8 = (bf16[256,1280]{1,0:T(8,128)(2,1)S(1)}, bf16[256,1280]{1,0:T(8,128)(2,1)}, u32[]{:S(2)}) copy-start(bf16[256,1280]{1,0:T(8,128)(2,1)} %copy-done.7) | copy-start | bytes 1966084
  138.4 6.2 %collective-permute-start.23 = (bf16[512,512]{1,0:T(8,128)(2,1)S(1)}, bf16[512,512]{1,0:T(8,128)(2,1)S(1)}, u32[]{:S(2)}, u32[]{:S(2)}) collective-permute-start(bf16[512,512]{1,0:T(8,128)(2,1)S(1)} %broadcast_select_fusion), channel_id=1, source_target_pairs={{0,2},{4,6},{8,10},{12,14},{16,18},{20,22},{24,26},{28,30},{32,34}... | collective-permute-start | bytes 1572872 | tf_op jit(solution)/shard_map/ppermute | solution.py:564
  139.8 9.8 %collective-permute-start.20 = (bf16[32,1408]{1,0:T(8,128)(2,1)S(1)}, bf16[32,1408]{1,0:T(8,128)(2,1)S(1)}, u32[]{:S(2)}, u32[]{:S(2)}) collective-permute-start(bf16[32,1408]{1,0:T(8,128)(2,1)S(1)} %get-tuple-element.97), channel_id=1, source_target_pairs={{0,16},{2,18},{4,20},{6,22},{8,24},{10,26},{12,28},{14,30},{16,0},... | collective-permute-start | bytes 270344 | tf_op jit(solution)/shard_map/ppermute | solution.py:471
  140.1 9.6 %collective-permute-start.21 = (bf16[32,1408]{1,0:T(8,128)(2,1)S(1)}, bf16[32,1408]{1,0:T(8,128)(2,1)S(1)}, u32[]{:S(2)}, u32[]{:S(2)}) collective-permute-start(bf16[32,1408]{1,0:T(8,128)(2,1)S(1)} %get-tuple-element.98), channel_id=1, source_target_pairs={{0,32},{2,34},{4,36},{6,38},{8,40},{10,42},{12,44},{14,46},{16,48}... | collective-permute-start | bytes 270344 | tf_op jit(solution)/shard_map/ppermute | solution.py:471
  140.1 9.6 %collective-permute-start.22 = (bf16[32,1408]{1,0:T(8,128)(2,1)S(1)}, bf16[32,1408]{1,0:T(8,128)(2,1)S(1)}, u32[]{:S(2)}, u32[]{:S(2)}) collective-permute-start(bf16[32,1408]{1,0:T(8,128)(2,1)S(1)} %get-tuple-element.99), channel_id=1, source_target_pairs={{0,48},{2,50},{4,52},{6,54},{8,56},{10,58},{12,60},{14,62},{16,32}... | collective-permute-start | bytes 270344 | tf_op jit(solution)/shard_map/ppermute | solution.py:471
  144.7 7.6 %copy-start.22 = (bf16[256,1280]{1,0:T(8,128)(2,1)S(1)}, bf16[256,1280]{1,0:T(8,128)(2,1)}, u32[]{:S(2)}) copy-start(bf16[256,1280]{1,0:T(8,128)(2,1)} %copy-done.21) | copy-start | bytes 1966084
  150.0 8.4 %collective-permute-start.24 = (bf16[16,1408]{1,0:T(8,128)(2,1)S(1)}, bf16[16,1408]{1,0:T(8,128)(2,1)S(1)}, u32[]{:S(2)}, u32[]{:S(2)}) collective-permute-start(bf16[16,1408]{1,0:T(8,128)(2,1)S(1)} %get-tuple-element.109), channel_id=1, source_target_pairs={{0,64},{2,66},{4,68},{6,70},{8,72},{10,74},{12,76},{14,78},{16,80}... | collective-permute-start | bytes 135176 | tf_op jit(solution)/shard_map/ppermute | solution.py:611
  (7 other events, 19.2 us)
